TPU v7x, 32 devices: a whole 2x2x4 slice. The times are simulated.
32 devices in a mesh: dp: 8 (over y, x, core), pipe: 4 (over z).
Axes of the slice: x: 2, y: 2, z: 4, core: 2. Of those that a mesh axis runs over, the one named last changes fastest.
Arguments:
- tokens: bfloat16 [16, 2048, 256], P('dp', 'pipe'), may hold values from -6 to 6
- segments: int32 [16, 2048], P('dp'), may hold values from 0 to 7, never falling along the last dimension, each value on 1 to 512 neighbouring positions
- cotangent: bfloat16 [16, 2048, 256], P('dp', 'pipe'), may hold values from -6 to 6
- attention_in: bfloat16 [2, 256, 768], replicated, may hold values from -0.5 to 0.5
- attention_in_bias: float32 [2, 512], replicated, may hold values from -3 to 3
- attention_out: bfloat16 [2, 256, 256], replicated, may hold values from -1.5 to 1.5
- attention_out_bias: float32 [2, 256], replicated, may hold values from -2 to 2
- attention_gain: float32 [2, 256], replicated, may hold values from 0.25 to 1.75
- attention_shift: float32 [2, 256], replicated, may hold values from -2 to 2
- expand_weight: bfloat16 [2, 256, 512], replicated, may hold values from -0.375 to 0.375
- expand_bias: float32 [2, 512], replicated, may hold values from -3 to 3
- contract_weight: bfloat16 [2, 512, 256], replicated, may hold values from -0.375 to 0.375
- contract_bias: float32 [2, 256], replicated, may hold values from -2 to 2
- feed_gain: float32 [2, 256], replicated, may hold values from 0.25 to 1.75
- feed_shift: float32 [2, 256], replicated, may hold values from -2 to 2
Outputs:
- layer_output: bfloat16 [16, 2048, 256], P('dp', 'pipe')
- input_grad: bfloat16 [16, 2048, 256], P('dp', 'pipe')
- gradient_attention_in: float32 [2, 256, 768], replicated
- gradient_attention_in_bias: float32 [2, 512], replicated
- gradient_attention_out: float32 [2, 256, 256], replicated
- gradient_attention_out_bias: float32 [2, 256], replicated
- gradient_attention_gain: float32 [2, 256], replicated
- gradient_attention_shift: float32 [2, 256], replicated
- gradient_expand_weight: float32 [2, 256, 512], replicated
- gradient_expand_bias: float32 [2, 512], replicated
- gradient_contract_weight: float32 [2, 512, 256], replicated
- gradient_contract_bias: float32 [2, 256], replicated
- gradient_feed_gain: float32 [2, 256], replicated
- gradient_feed_shift: float32 [2, 256], replicated
Inputs may be any that keep to these rules, and one draw needn't show every extreme that they name: `segments`: along a row the numbers never fall; each of the 8 numbers marks one document of 1 to 512 consecutive positions, and some document has exactly 512.
All inputs are finite; a program needn't handle non-finite values.
Results may differ from a plain program's by a relative error of at most 0.03.
The roundings to bfloat16 on the way count: a program that leaves them out, or rounds other values in their place, can miss the bound.
Values may be sent and summed in bfloat16 or wider, within the bound.
No kernel may reach another device: no remote copies, remote signals or barrier semaphores. Data moves between devices by JAX's collectives and lax.ppermute only.
A program may use at most 192 MiB of HBM per device.

v0:
```python
import jax
import jax.numpy as jnp
from jax import lax
from jax.sharding import PartitionSpec as P

HEADS = 4


EPSILON = 1e-12
MASKED = -1e30


def passed_along(value, axis, by):
    count = lax.axis_size(axis)
    pairs = [(i, i + by) for i in range(count) if 0 <= i + by < count]
    return lax.ppermute(value, axis, pairs)


def normalize(values, norm_gain, norm_shift):
    average = jnp.mean(values, axis=-1, keepdims=True)
    centred = values - average
    spread = jnp.mean(centred * centred, axis=-1, keepdims=True)
    return centred * lax.rsqrt(spread + EPSILON) * norm_gain + norm_shift


def gelu_exact(values):
    return jax.nn.gelu(values, approximate=False)


def masked_scores(query_block, key_heads, seg_query, seg_keys, scaling):
    scores = (
        jnp.einsum("qhd,khd->hqk", query_block, key_heads, preferred_element_type=jnp.float32)
        * scaling
    )
    return jnp.where((seg_query[:, None] == seg_keys[None, :])[None], scores, MASKED)


def context_sweep(query_heads, key_heads, value_heads, seg_queries, seg_keys, scaling, kept_logs):
    length, head_count, head_size = query_heads.shape
    block_rows = min(512, length)

    def context_one_block(block_index):
        offset = block_index * block_rows
        query_block = lax.dynamic_slice_in_dim(query_heads, offset, block_rows, 0)
        seg_query = lax.dynamic_slice_in_dim(seg_queries, offset, block_rows, 0)
        scores = masked_scores(query_block, key_heads, seg_query, seg_keys, scaling)
        if kept_logs is None:
            highest = jnp.max(scores, axis=-1, keepdims=True)
            log_total = highest[..., 0] + jnp.log(jnp.sum(jnp.exp(scores - highest), axis=-1))
        else:
            log_total = lax.dynamic_slice_in_dim(kept_logs, offset, block_rows, 1)
        weights_low = jnp.exp(scores - log_total[..., None]).astype(jnp.bfloat16)
        context = jnp.einsum(
            "hqk,khd->qhd", weights_low, value_heads, preferred_element_type=jnp.float32
        )
        return (context, log_total)

    context, log_total = lax.map(context_one_block, jnp.arange(length // block_rows))
    context = context.reshape(length, head_count * head_size)
    log_total = jnp.transpose(log_total, (1, 0, 2)).reshape(head_count, length)
    return (context, log_total)


def gradient_sweep(
    query_heads, key_heads, value_heads, seg_queries, seg_keys, scaling, kept_logs, context_grad
):
    length, head_count, head_size = query_heads.shape
    block_rows = min(512, length)

    def gradient_one_block(running_total, block_index):
        key_grads, value_grads = running_total
        offset = block_index * block_rows
        query_block = lax.dynamic_slice_in_dim(query_heads, offset, block_rows, 0)
        seg_query = lax.dynamic_slice_in_dim(seg_queries, offset, block_rows, 0)
        log_total = lax.dynamic_slice_in_dim(kept_logs, offset, block_rows, 1)
        context_block = lax.dynamic_slice_in_dim(context_grad, offset, block_rows, 0)
        scores = masked_scores(query_block, key_heads, seg_query, seg_keys, scaling)
        weights_full = jnp.exp(scores - log_total[..., None])
        weights_low = weights_full.astype(jnp.bfloat16)
        weight_grads = jnp.einsum(
            "qhd,khd->hqk", context_block, value_heads, preferred_element_type=jnp.float32
        )
        inner = jnp.sum(weights_full * weight_grads, axis=-1, keepdims=True)
        score_grads = (weights_full * (weight_grads - inner)).astype(jnp.bfloat16)
        query_grads = (
            jnp.einsum("hqk,khd->qhd", score_grads, key_heads, preferred_element_type=jnp.float32)
            * scaling
        )
        key_grads = (
            key_grads
            + jnp.einsum(
                "hqk,qhd->khd", score_grads, query_block, preferred_element_type=jnp.float32
            )
            * scaling
        )
        value_grads = value_grads + jnp.einsum(
            "hqk,qhd->khd", weights_low, context_block, preferred_element_type=jnp.float32
        )
        return ((key_grads, value_grads), query_grads)

    key_zero = jnp.zeros(key_heads.shape, jnp.float32)
    (key_grads, value_grads), query_grads = lax.scan(
        gradient_one_block, (key_zero, key_zero), jnp.arange(length // block_rows)
    )
    features = head_count * head_size
    return (
        query_grads.reshape(length, features),
        key_grads.reshape(-1, features),
        value_grads.reshape(-1, features),
    )


def unchanged(values):
    return values


def attend_project(hidden, params):
    row_count, length, features = hidden.shape
    bias_full = jnp.concatenate(
        [params[1][:features], jnp.zeros((features,), jnp.float32), params[1][features:]]
    )
    joined_qkv = (
        jnp.dot(hidden.reshape(-1, features), params[0], preferred_element_type=jnp.float32)
        + bias_full
    ).astype(jnp.bfloat16)
    joined_qkv = joined_qkv.reshape(row_count, length, 3 * features)
    return (joined_qkv[..., :features], joined_qkv[..., features:])


def split_heads(query_row, pair_row, features):
    head_size = features // HEADS
    query_heads = query_row.reshape(-1, HEADS, head_size)
    key_heads = pair_row[:, :features].reshape(-1, HEADS, head_size)
    value_heads = pair_row[:, features:].reshape(-1, HEADS, head_size)
    return (query_heads, key_heads, value_heads)


def rows_context(queries, pair, seg_queries, seg_keys, kept_logs):
    features = queries.shape[2]
    scaling = (features // HEADS) ** (-0.5)
    contexts = []
    logs = []
    for row in range(queries.shape[0]):
        query_heads, key_heads, value_heads = split_heads(queries[row], pair[row], features)
        row_logs = None if kept_logs is None else kept_logs[row]
        context, log_total = context_sweep(
            query_heads, key_heads, value_heads, seg_queries[row], seg_keys[row], scaling, row_logs
        )
        contexts.append(context)
        logs.append(log_total)
    return (jnp.stack(contexts), jnp.stack(logs))


def attend_forward(hidden, seg_queries, seg_keys, params, widen):
    features = hidden.shape[2]
    queries, pair = attend_project(hidden, params)
    pair = widen(pair)
    context, log_total = rows_context(queries, pair, seg_queries, seg_keys, None)
    flat_hidden = hidden.reshape(-1, features)
    summed = (
        flat_hidden.astype(jnp.float32)
        + jnp.dot(
            context.reshape(-1, features).astype(jnp.bfloat16),
            params[2],
            preferred_element_type=jnp.float32,
        )
        + params[3]
    )
    return (normalize(summed, params[4], params[5]).reshape(hidden.shape), log_total)


def attend_backward(
    hidden, incoming_gradient, seg_queries, seg_keys, kept_logs, params, widen, narrow
):
    weight_in, bias_in, weight_out, bias_out, norm_gain, norm_shift = params
    row_count, length, features = hidden.shape
    head_size = features // HEADS
    scaling = head_size ** (-0.5)
    queries, pair = attend_project(hidden, params)
    pair = widen(pair)
    context_low = (
        rows_context(queries, pair, seg_queries, seg_keys, kept_logs)[0]
        .reshape(-1, features)
        .astype(jnp.bfloat16)
    )
    flat_hidden = hidden.reshape(-1, features)
    summed = (
        flat_hidden.astype(jnp.float32)
        + jnp.dot(context_low, weight_out, preferred_element_type=jnp.float32)
        + bias_out
    )
    norm_pull = jax.vjp(normalize, summed, norm_gain, norm_shift)[1]
    sum_grad, gain_grad, shift_grad = norm_pull(
        incoming_gradient.reshape(-1, features).astype(jnp.float32)
    )
    branch_grad = sum_grad.astype(jnp.bfloat16)
    weight_out_grad = jnp.einsum(
        "sd,se->de", context_low, branch_grad, preferred_element_type=jnp.float32
    )
    bias_out_grad = jnp.sum(branch_grad.astype(jnp.float32), axis=0)
    context_grad = jnp.einsum(
        "se,de->sd", branch_grad, weight_out, preferred_element_type=jnp.float32
    ).astype(jnp.bfloat16)
    context_grad = context_grad.reshape(row_count, length, HEADS, head_size)
    query_list = []
    pair_list = []
    for row in range(row_count):
        query_heads, key_heads, value_heads = split_heads(queries[row], pair[row], features)
        query_grad, key_grad, value_grad = gradient_sweep(
            query_heads,
            key_heads,
            value_heads,
            seg_queries[row],
            seg_keys[row],
            scaling,
            kept_logs[row],
            context_grad[row],
        )
        query_list.append(query_grad)
        pair_list.append(jnp.concatenate([key_grad, value_grad], axis=1))
    pair_grads = narrow(jnp.stack(pair_list))
    joined_grad = (
        jnp.concatenate([jnp.stack(query_list), pair_grads], axis=2)
        .astype(jnp.bfloat16)
        .reshape(-1, 3 * features)
    )
    weight_in_grad = jnp.einsum(
        "sd,se->de", flat_hidden, joined_grad, preferred_element_type=jnp.float32
    )
    column_sums = jnp.sum(joined_grad.astype(jnp.float32), axis=0)
    bias_in_grad = jnp.concatenate([column_sums[:features], column_sums[2 * features :]])
    hidden_grad = (
        jnp.einsum("se,de->sd", joined_grad, weight_in, preferred_element_type=jnp.float32)
        + sum_grad
    )
    return (
        hidden_grad.reshape(hidden.shape),
        (weight_in_grad, bias_in_grad, weight_out_grad, bias_out_grad, gain_grad, shift_grad),
    )


def expand_forward(hidden, params):
    pre_up = jnp.dot(hidden, params[0], preferred_element_type=jnp.float32) + params[1]
    active = gelu_exact(pre_up).astype(jnp.bfloat16)
    summed = (
        hidden.astype(jnp.float32)
        + jnp.dot(active, params[2], preferred_element_type=jnp.float32)
        + params[3]
    )
    return normalize(summed, params[4], params[5])


def expand_backward(hidden, incoming_gradient, params):
    weight_up, bias_up, weight_down, bias_down, norm_gain, norm_shift = params
    pre_up = jnp.dot(hidden, weight_up, preferred_element_type=jnp.float32) + bias_up
    active_full, gelu_pull = jax.vjp(gelu_exact, pre_up)
    active = active_full.astype(jnp.bfloat16)
    summed = (
        hidden.astype(jnp.float32)
        + jnp.dot(active, weight_down, preferred_element_type=jnp.float32)
        + bias_down
    )
    norm_pull = jax.vjp(normalize, summed, norm_gain, norm_shift)[1]
    sum_grad, gain_grad, shift_grad = norm_pull(incoming_gradient.astype(jnp.float32))
    branch_grad = sum_grad.astype(jnp.bfloat16)
    weight_down_grad = jnp.einsum(
        "sf,sd->fd", active, branch_grad, preferred_element_type=jnp.float32
    )
    bias_down_grad = jnp.sum(branch_grad.astype(jnp.float32), axis=0)
    active_grad = jnp.einsum(
        "sd,fd->sf", branch_grad, weight_down, preferred_element_type=jnp.float32
    )
    pre_grad = gelu_pull(active_grad)[0].astype(jnp.bfloat16)
    up_weight_gradient = jnp.einsum(
        "sd,sf->df", hidden, pre_grad, preferred_element_type=jnp.float32
    )
    bias_up_grad = jnp.sum(pre_grad.astype(jnp.float32), axis=0)
    hidden_grad = (
        jnp.einsum("sf,df->sd", pre_grad, weight_up, preferred_element_type=jnp.float32) + sum_grad
    )
    return (
        hidden_grad,
        (up_weight_gradient, bias_up_grad, weight_down_grad, bias_down_grad, gain_grad, shift_grad),
    )


def pick_layer(sources, layer_position):
    return tuple(
        (lax.dynamic_index_in_dim(source, layer_position, 0, keepdims=False) for source in sources)
    )


def layer_zeros(sources):
    return tuple((jnp.zeros(source.shape[1:], jnp.float32) for source in sources))


def full_zeros(sources):
    return tuple((jnp.zeros(source.shape, jnp.float32) for source in sources))


def accumulate_layer(layer_totals, summand_terms, layer_position):
    return tuple(
        (
            running_total.at[layer_position].add(summand_term)
            for running_total, summand_term in zip(layer_totals, summand_terms)
        )
    )


def keep_slot(stored, slot_index, active, update):
    return stored.at[slot_index].set(jnp.where(active, update, stored[slot_index]))


def body(
    tokens,
    segments,
    cotangent,
    attention_in,
    attention_in_bias,
    attention_out,
    attention_out_bias,
    attention_gain,
    attention_shift,
    expand_weight,
    expand_bias,
    contract_weight,
    contract_bias,
    feed_gain,
    feed_shift,
):
    attend_params = (
        attention_in,
        attention_in_bias,
        attention_out,
        attention_out_bias,
        attention_gain,
        attention_shift,
    )
    expand_params = (
        expand_weight,
        expand_bias,
        contract_weight,
        contract_bias,
        feed_gain,
        feed_shift,
    )
    section_count = lax.axis_size("pipe")
    section_index = lax.axis_index("pipe")
    micro_count = tokens.shape[0]
    features = tokens.shape[2]
    length = segments.shape[1]
    zero_rows = jnp.zeros((micro_count, length, features), jnp.float32)
    zero_hidden = jnp.zeros((length, features), jnp.float32)
    zero_logs = jnp.zeros((HEADS, length), jnp.float32)
    attend_zero = layer_zeros(attend_params)
    expand_zero = layer_zeros(expand_params)
    attend_totals = full_zeros(attend_params)
    expand_totals = full_zeros(expand_params)
    inputs_all, cotangent_all = (
        lax.all_gather(tokens, "pipe", axis=1, tiled=True),
        lax.all_gather(cotangent, "pipe", axis=1, tiled=True),
    )
    layer_position = section_index // 2
    section_kind = section_index % 2
    attend_own = pick_layer(attend_params, layer_position)
    expand_own = pick_layer(expand_params, layer_position)

    def run_attend(hidden, seg_row):
        result, log_total = attend_forward(
            hidden[None], seg_row[None], seg_row[None], attend_own, unchanged
        )
        return (result[0], log_total[0])

    def run_expand(hidden, seg_row):
        return (expand_forward(hidden, expand_own), zero_logs)

    def run_spare(hidden, seg_row):
        return (zero_hidden, zero_logs)

    step_count = micro_count + section_count - 1
    received = jnp.zeros((length, features), jnp.bfloat16)
    kept_inputs = jnp.zeros((micro_count, length, features), jnp.bfloat16)
    kept_logs = jnp.zeros((micro_count, HEADS, length), jnp.float32)
    last_outputs = zero_rows
    for moment in range(step_count):
        micro_index = moment - section_index
        active = (micro_index >= 0) & (micro_index < micro_count)
        slot_index = jnp.clip(micro_index, 0, micro_count - 1)
        hidden = jnp.where(section_index == 0, inputs_all[slot_index], received)
        branch = jnp.where(active, section_kind, 2)
        result, log_total = lax.switch(
            branch, [run_attend, run_expand, run_spare], hidden, segments[slot_index]
        )
        kept_inputs = keep_slot(kept_inputs, slot_index, active, hidden)
        kept_logs = keep_slot(kept_logs, slot_index, active, log_total)
        last_outputs = keep_slot(last_outputs, slot_index, active, result)
        if moment + 1 < step_count:
            received = passed_along(result.astype(jnp.bfloat16), "pipe", 1)

    def back_attend(hidden, incoming_gradient, seg_row, log_total):
        hidden_grad, layer_terms = attend_backward(
            hidden[None],
            incoming_gradient[None],
            seg_row[None],
            seg_row[None],
            log_total[None],
            attend_own,
            unchanged,
            unchanged,
        )
        return (hidden_grad[0], layer_terms, expand_zero)

    def back_expand(hidden, incoming_gradient, seg_row, log_total):
        hidden_grad, layer_terms = expand_backward(hidden, incoming_gradient, expand_own)
        return (hidden_grad, attend_zero, layer_terms)

    def back_spare(hidden, incoming_gradient, seg_row, log_total):
        return (zero_hidden, attend_zero, expand_zero)

    received_grad = jnp.zeros((length, features), jnp.bfloat16)
    input_grads = zero_rows
    for moment in range(step_count):
        micro_index = moment - (section_count - 1 - section_index)
        active = (micro_index >= 0) & (micro_index < micro_count)
        slot_index = jnp.clip(micro_index, 0, micro_count - 1)
        incoming_gradient = jnp.where(
            section_index == section_count - 1, cotangent_all[slot_index], received_grad
        )
        branch = jnp.where(active, section_kind, 2)
        hidden_grad, attend_terms, expand_terms = lax.switch(
            branch,
            [back_attend, back_expand, back_spare],
            kept_inputs[slot_index],
            incoming_gradient,
            segments[slot_index],
            kept_logs[slot_index],
        )
        attend_totals = accumulate_layer(attend_totals, attend_terms, layer_position)
        expand_totals = accumulate_layer(expand_totals, expand_terms, layer_position)
        input_grads = keep_slot(input_grads, slot_index, active, hidden_grad)
        if moment + 1 < step_count:
            received_grad = passed_along(hidden_grad.astype(jnp.bfloat16), "pipe", -1)
    output_terms = jnp.where(section_index == section_count - 1, last_outputs, 0.0)
    input_terms = jnp.where(section_index == 0, input_grads, 0.0)
    layer_output, input_grad = (
        lax.psum_scatter(
            output_terms.astype(jnp.bfloat16), "pipe", scatter_dimension=1, tiled=True
        ).astype(jnp.float32),
        lax.psum_scatter(
            input_terms.astype(jnp.bfloat16), "pipe", scatter_dimension=1, tiled=True
        ).astype(jnp.float32),
    )
    in_total, in_bias_total, out_total, out_bias_total, attend_gain_total, attend_shift_total = (
        attend_totals
    )
    up_total, up_bias_total, down_total, down_bias_total, feed_gain_total, feed_shift_total = (
        expand_totals
    )
    summed_grads = lax.psum(
        (
            in_total,
            in_bias_total,
            out_total,
            out_bias_total,
            attend_gain_total,
            attend_shift_total,
            up_total,
            up_bias_total,
            down_total,
            down_bias_total,
            feed_gain_total,
            feed_shift_total,
        ),
        ("dp", "pipe"),
    )
    return (layer_output.astype(jnp.bfloat16), input_grad.astype(jnp.bfloat16)) + tuple(
        summed_grads
    )


def solution(mesh):
    placed = (
        P("dp", "pipe", None),
        P("dp", None),
        P("dp", "pipe", None),
        P(),
        P(),
        P(),
        P(),
        P(),
        P(),
        P(),
        P(),
        P(),
        P(),
        P(),
        P(),
    )
    return jax.shard_map(
        body,
        mesh=mesh,
        in_specs=placed,
        out_specs=(
            P("dp", "pipe", None),
            P("dp", "pipe", None),
            P(),
            P(),
            P(),
            P(),
            P(),
            P(),
            P(),
            P(),
            P(),
            P(),
            P(),
            P(),
        ),
        check_vma=False,
    )
```

profile of v0, /device:TPU:0, one launch (start us, length us, event | category | flops | bytes accessed | tf_op | source)
XLA Modules:
  0.0 1751.4 jit_solution(18087535892462489239)
XLA Ops:
  22.1 36.3 %all-gather.3.cloned.1.call-done = bf16[2,2048,256]{2,1,0:T(8,128)(2,1)} async-done(((bf16[2,512,256]{2,1,0:T(8,128)(2,1)}), bf16[2,2048,256]{2,1,0:T(8,128)(2,1)}) %all-gather.3.cloned.1.call-update) | async-done | bytes 2097168 | tf_op jit(solution)/shard_map/all_gather | solution.py:360
  63.0 79.1 %conditional.10 = (f32[4,2048]{1,0:T(4,128)S(1)}, bf16[2048,256]{1,0:T(8,128)(2,1)}) conditional(s32[]{:T(128)} %clamp.30, (bf16[2048,256]{1,0:T(8,128)(2,1)S(1)}, bf16[256,768]{1,0:T(8,128)(2,1)}, f32[512]{0:T(512)S(1)}, s32[2,2048]{1,0:T(2,128)S(1)}, s32[]{:T(128)}, /*index=5*/bf16[256,256]{1,0:T(8,128)(2,1)S(1)}, ...), branch_computations={%region_1.8_spmd, %region_8.11_spmd, %region_11.12_spmd} | conditional | flops 2204108288 | bytes 107404760 | solution.py:391
  68.0 59.9 %while.350 = (s32[]{:T(128)}, bf16[4,512,4,64]{1,3,2,0:T(8,128)(2,1)}, f32[4,4,512]{2,1,0:T(4,128)S(1)}, s32[4]{0:T(128)S(1)}, s32[2048]{0:T(1024)S(1)}, /*index...) while((s32[]{:T(128)}, ...), condition=%wide.region_5.5_spmd, body=%wide.region_2.4_spmd.sunk | while | flops 1120925696 | bytes 70072616 | solution.py:58
  170.1 79.2 %conditional.11 = (f32[4,2048]{1,0:T(4,128)S(1)}, bf16[2048,256]{1,0:T(8,128)(2,1)S(1)}) conditional(s32[]{:T(128)} %clamp.31, (bf16[2048,256]{1,0:T(8,128)(2,1)}, bf16[256,768]{1,0:T(8,128)(2,1)}, f32[512]{0:T(512)S(1)}, s32[2,2048]{1,0:T(2,128)S(1)}, s32[]{:T(128)}, /*index=5*/bf16[256,256]{1,0:T(8,128)(2,1)S(1)}, ...), branch_computations={%region_13.20_spmd, %region_20.23_spmd, %region_23.24_spmd} | conditional | flops 2204108288 | bytes 107404760 | solution.py:391
  176.3 59.5 %while.351 = (s32[]{:T(128)}, bf16[4,512,4,64]{1,3,2,0:T(8,128)(2,1)}, f32[4,4,512]{2,1,0:T(4,128)S(1)}, s32[4]{0:T(128)S(1)}, s32[2048]{0:T(1024)S(1)}, /*index...) while((s32[]{:T(128)}, ...), condition=%wide.region_17.17_spmd, body=%wide.region_14.16_spmd.sunk | while | flops 1120925696 | bytes 70072616 | solution.py:58
  260.2 12.6 collective-permute-done.1
  284.3 12.3 collective-permute-start.2
  306.0 11.7 collective-permute-done.2
  375.5 23.3 %conditional.15 = (f32[256,768]{1,0:T(8,128)S(1)}, f32[512]{0:T(512)S(1)}, f32[256,256]{1,0:T(8,128)}, f32[256]{0:T(256)}, f32[256]{0:T(256)}, /*index=5*/f32[25...) conditional(s32[]{:T(128)} %clamp.35, ...), branch_computations={%region_62.76_spmd, %region_76.85_spmd, %region_85.86_spmd} | conditional | flops 7121543680 | bytes 328645184 | solution.py:430
  420.5 94.3 %collective-permute-done.4 = bf16[2048,256]{1,0:T(8,128)(2,1)} collective-permute-done((bf16[2048,256]{1,0:T(8,128)(2,1)}, bf16[2048,256]{1,0:T(8,128)(2,1)}, u32[]{:S(2)}, u32[]{:S(2)}) %collective-permute-start.4) | collective-permute-done | bytes 1048608 | tf_op jit(solution)/shard_map/ppermute | solution.py:16
  516.4 19.6 %conditional.16 = (f32[256]{0:T(256)}, f32[256]{0:T(256)S(1)}, f32[256]{0:T(256)S(1)}, f32[1,256,768]{2,1,0:T(8,128)S(1)}, f32[1,512]{1,0:T(1,128)S(1)}, /*index...) conditional(s32[]{:T(128)} %clamp.36, ...), branch_computations={%region_87.101_spmd, %region_101.110_spmd, %region_110.111_spmd} | conditional | flops 7121543680 | bytes 328645184 | solution.py:430
  565.8 19.5 %conditional.17 = (f32[256]{0:T(256)}, f32[256]{0:T(256)S(1)}, f32[256]{0:T(256)S(1)}, f32[1,256,768]{2,1,0:T(8,128)S(1)}, f32[1,512]{1,0:T(1,128)S(1)}, /*index...) conditional(s32[]{:T(128)} %clamp.37, ...), branch_computations={%region_112.126_spmd, %region_126.135_spmd, %region_135.136_spmd} | conditional | flops 7121543680 | bytes 328645184 | solution.py:430
  606.7 310.2 %collective-permute-done.6 = bf16[2048,256]{1,0:T(8,128)(2,1)S(1)} collective-permute-done((bf16[2048,256]{1,0:T(8,128)(2,1)}, bf16[2048,256]{1,0:T(8,128)(2,1)S(1)}, u32[]{:S(2)}, u32[]{:S(2)}) %collective-permute-start.6) | collective-permute-done | bytes 1048608 | tf_op jit(solution)/shard_map/ppermute | solution.py:16
  917.2 285.7 %conditional.18 = (f32[256]{0:T(256)}, f32[256]{0:T(256)S(1)}, f32[256]{0:T(256)S(1)}, f32[1,256,768]{2,1,0:T(8,128)S(1)}, f32[1,512]{1,0:T(1,128)S(1)}, /*index...) conditional(s32[]{:T(128)} %clamp.38, ...), branch_computations={%region_137.151_spmd, %region_151.160_spmd, %region_160.161_spmd} | conditional | flops 7121543680 | bytes 328645184 | solution.py:430
  928.6 49.1 %while.361 = (s32[]{:T(128)}, bf16[4,512,4,64]{1,3,2,0:T(8,128)(2,1)}, s32[4]{0:T(128)S(1)}, s32[2048]{0:T(1024)S(1)}, s32[1,2048]{1,0:T(1,128)S(1)}, /*index=5*...) while((s32[]{:T(128)}, ...), condition=%wide.region_139.139_spmd, body=%wide.region_138.138_spmd.sunk | while | flops 1091567616 | bytes 6068431 | solution.py:58
  989.4 189.8 %while.362 = (s32[]{:T(128)}, f32[2048,4,64]{0,2,1:T(8,128)}, f32[2048,4,64]{0,2,1:T(8,128)}, bf16[4,512,4,64]{1,3,2,0:T(8,128)(2,1)}, s32[4]{0:T(128)S(1)}, /*i...) while((s32[]{:T(128)}, f32[2048,4,64]{0,2,1:T(8,128)}, ...), condition=%wide.region_146.146_spmd.clone, body=%wide.region_144.145_spmd.clone.sunk | while | flops 2751068160 | bytes 197728656 | solution.py:102
  1216.1 29.3 %collective-permute-done.7 = bf16[2048,256]{1,0:T(8,128)(2,1)} collective-permute-done((bf16[2048,256]{1,0:T(8,128)(2,1)}, bf16[2048,256]{1,0:T(8,128)(2,1)}, u32[]{:S(2)}, u32[]{:S(2)}) %collective-permute-start.7) | collective-permute-done | bytes 1048608 | tf_op jit(solution)/shard_map/ppermute | solution.py:16
  1246.9 294.1 %conditional.19 = (f32[256]{0:T(256)}, f32[256]{0:T(256)S(1)}, f32[256]{0:T(256)S(1)}, f32[1,256,768]{2,1,0:T(8,128)S(1)}, f32[1,512]{1,0:T(1,128)S(1)}, /*index...) conditional(s32[]{:T(128)} %clamp.39, ...), branch_computations={%region_162.176_spmd, %region_176.185_spmd, %region_185.186_spmd} | conditional | flops 7121543680 | bytes 328645184 | solution.py:430
  1257.8 63.3 %while.363 = (s32[]{:T(128)}, bf16[4,512,4,64]{1,3,2,0:T(8,128)(2,1)}, s32[4]{0:T(128)S(1)}, s32[2048]{0:T(1024)S(1)}, s32[1,2048]{1,0:T(1,128)S(1)}, /*index=5*...) while((s32[]{:T(128)}, ...), condition=%wide.region_164.164_spmd, body=%wide.region_163.163_spmd.sunk | while | flops 1091567616 | bytes 6068431 | solution.py:58
  1332.7 189.3 %while.364 = (s32[]{:T(128)}, f32[2048,4,64]{0,2,1:T(8,128)}, f32[2048,4,64]{0,2,1:T(8,128)}, bf16[4,512,4,64]{1,3,2,0:T(8,128)(2,1)}, s32[4]{0:T(128)S(1)}, /*i...) while((s32[]{:T(128)}, f32[2048,4,64]{0,2,1:T(8,128)}, ...), condition=%wide.region_171.171_spmd.clone, body=%wide.region_169.170_spmd.clone.sunk | while | flops 2751068160 | bytes 197728656 | solution.py:102
  1440.6 11.1 multiply_reduce_fusion.30
  1571.3 38.7 %all-reduce = (f32[2,512]{1,0:T(2,128)}, f32[2,256]{1,0:T(2,128)}, f32[2,256]{1,0:T(2,128)}, f32[2,256]{1,0:T(2,128)}, f32[2,512]{1,0:T(2,128)}, /*index=5*/f32[...) all-reduce(f32[2,512]{1,0:T(2,128)S(1)} %scatter-add.215, ...), channel_id=1, replica_groups=mesh['dp'=8,'pipe'=4] {'dp','pipe'}, use_global_device_ids=true, to_apply=%region_190.191 | all-reduce | flops 5120 | bytes 40960 | tf_op jit(solution)/shard_map/psum | solution.py:459
  1610.0 82.9 %all-reduce.4.cloned.1.call-done = (f32[2,256,768]{2,1,0:T(8,128)}, f32[2,256,256]{2,1,0:T(8,128)}, f32[2,256,512]{2,1,0:T(8,128)}, f32[2,512,256]{2,1,0:T(8,128)}) async-done(((f32[2,256,768]{2,1,0:T(8,128)}, f32[2,256,256]{2,1,0:T(8,128)}, f32[2,256,512]{2,1,0:T(8,128)}, f32[2,512,256]{2,1,0:T(8,128)}), (f32[2,256,768]{2,1,0:T(8,128)}, f32[2,256,256]{2,1,0:T(8,128)}, f32[2,256,512]{2,1,0:T(8,128)}, ...) | async-done | bytes 4194320 | tf_op jit(solution)/shard_map/psum | solution.py:459
  1692.9 45.3 %reduce-scatter.5.cloned.1.call-done = bf16[2,512,256]{2,1,0:T(8,128)(2,1)} async-done(((bf16[2,2048,256]{2,1,0:T(8,128)(2,1)}), bf16[2,512,256]{2,1,0:T(8,128)(2,1)}) %reduce-scatter.5.cloned.1.call-update) | async-done | bytes 524304 | tf_op jit(solution)/shard_map/reduce_scatter | solution.py:449
  (1051 shorter events, 936.0 us)
Async XLA Ops:
  7.2 51.1 %all-gather.3.cloned.1.call-start = ((), (), s32[]{:S(2)}) async-start(), calls=%async_computation.2 | async-start | bytes 2621440 | tf_op jit(solution)/shard_map/all_gather | solution.py:360
  7.9 145.7 %all-gather.5.cloned.1.call-start = ((), (), s32[]{:S(2)}) async-start(), calls=%async_computation.4 | async-start | bytes 2621440 | tf_op jit(solution)/shard_map/all_gather | solution.py:361
  8.7 1601.3 %reduce-scatter.3.cloned.1.call-start = ((), (), s32[]{:S(2)}) async-start(), calls=%async_computation.3 | async-start | bytes 2621440 | tf_op jit(solution)/shard_map/reduce_scatter | solution.py:446
  9.6 365.9 %copy-start.139 = (f32[1,256]{1,0:T(1,128)}, f32[1,256]{1,0:T(1,128)S(1)}, u32[]{:S(2)}) copy-start(f32[1,256]{1,0:T(1,128)S(1)} %get-tuple-element.4143) | copy-start | bytes 3076
  9.6 506.7 %copy-start.179 = (f32[1,256]{1,0:T(1,128)}, f32[1,256]{1,0:T(1,128)S(1)}, u32[]{:S(2)}) copy-start(f32[1,256]{1,0:T(1,128)S(1)} %get-tuple-element.4144) | copy-start | bytes 3076
  11.0 505.3 %copy-start.154 = (f32[1,256]{1,0:T(1,128)}, f32[1,256]{1,0:T(1,128)S(1)}, u32[]{:S(2)}) copy-start(f32[1,256]{1,0:T(1,128)S(1)} %get-tuple-element.4139) | copy-start | bytes 3076
  11.0 505.3 %copy-start.210 = (f32[1,256]{1,0:T(1,128)}, f32[1,256]{1,0:T(1,128)S(1)}, u32[]{:S(2)}) copy-start(f32[1,256]{1,0:T(1,128)S(1)} %get-tuple-element.4140) | copy-start | bytes 3076
  11.7 504.6 %copy-start.161 = (f32[1,512]{1,0:T(1,128)}, f32[1,512]{1,0:T(1,128)S(1)}, u32[]{:S(2)}) copy-start(f32[1,512]{1,0:T(1,128)S(1)} %get-tuple-element.4142) | copy-start | bytes 6148
  11.7 504.6 %copy-start.284 = (f32[1,512]{1,0:T(1,128)}, f32[1,512]{1,0:T(1,128)S(1)}, u32[]{:S(2)}) copy-start(f32[1,512]{1,0:T(1,128)S(1)} %get-tuple-element.4141) | copy-start | bytes 6148
  18.4 357.1 %copy-start.37 = (bf16[256,256]{1,0:T(8,128)(2,1)}, bf16[256,256]{1,0:T(8,128)(2,1)S(1)}, u32[]{:S(2)}) copy-start(bf16[256,256]{1,0:T(8,128)(2,1)S(1)} %dynamic-slice_bitcast_fusion.8) | copy-start | bytes 393220
  21.2 354.4 %copy-start.89 = (bf16[512,256]{1,0:T(8,128)(2,1)}, bf16[512,256]{1,0:T(8,128)(2,1)S(1)}, u32[]{:S(2)}) copy-start(bf16[512,256]{1,0:T(8,128)(2,1)S(1)} %dynamic-slice_bitcast_fusion.6) | copy-start | bytes 786436
  142.1 24.3 %collective-permute-start = (bf16[2048,256]{1,0:T(8,128)(2,1)}, bf16[2048,256]{1,0:T(8,128)(2,1)}, u32[]{:S(2)}, u32[]{:S(2)}) collective-permute-start(bf16[2048,256]{1,0:T(8,128)(2,1)} %get-tuple-element.3545), channel_id=1, source_target_pairs={{0,1},{1,2},{2,3},{4,5},{5,6},{6,7},{8,9},{9,10},{10,11},{12,13},{... | collective-permute-start | bytes 3145736 | tf_op jit(solution)/shard_map/ppermute | solution.py:16
  249.3 23.5 %collective-permute-start.1 = (bf16[2048,256]{1,0:T(8,128)(2,1)S(1)}, bf16[2048,256]{1,0:T(8,128)(2,1)S(1)}, u32[]{:S(2)}, u32[]{:S(2)}) collective-permute-start(bf16[2048,256]{1,0:T(8,128)(2,1)S(1)} %get-tuple-element.3546), channel_id=1, source_target_pairs={{0,1},{1,2},{2,3},{4,5},{5,6},{6,7},{8,9},{9,10},{10,11},{12,13},{... | collective-permute-start | bytes 3145736 | tf_op jit(solution)/shard_map/ppermute | solution.py:16
  284.3 33.4 %collective-permute-start.2 = (bf16[2048,256]{1,0:T(8,128)(2,1)S(1)}, bf16[2048,256]{1,0:T(8,128)(2,1)S(1)}, u32[]{:S(2)}, u32[]{:S(2)}) collective-permute-start(bf16[2048,256]{1,0:T(8,128)(2,1)S(1)} %get-tuple-element.3547), channel_id=1, source_target_pairs={{0,1},{1,2},{2,3},{4,5},{5,6},{6,7},{8,9},{9,10},{10,11},{12,13},{... | collective-permute-start | bytes 3145736 | tf_op jit(solution)/shard_map/ppermute | solution.py:16
  329.2 25.1 %collective-permute-start.3 = (bf16[2048,256]{1,0:T(8,128)(2,1)S(1)}, bf16[2048,256]{1,0:T(8,128)(2,1)S(1)}, u32[]{:S(2)}, u32[]{:S(2)}) collective-permute-start(bf16[2048,256]{1,0:T(8,128)(2,1)S(1)} %get-tuple-element.3548), channel_id=1, source_target_pairs={{0,1},{1,2},{2,3},{4,5},{5,6},{6,7},{8,9},{9,10},{10,11},{12,13},{... | collective-permute-start | bytes 3145736 | tf_op jit(solution)/shard_map/ppermute | solution.py:16
  369.5 1323.4 %all-reduce.4.cloned.1.call-start = ((), (), s32[]{:S(2)}) async-start(), calls=%async_computation.6 | async-start | bytes 8388608 | tf_op jit(solution)/shard_map/psum | solution.py:459
  406.5 108.3 %collective-permute-start.4 = (bf16[2048,256]{1,0:T(8,128)(2,1)}, bf16[2048,256]{1,0:T(8,128)(2,1)}, u32[]{:S(2)}, u32[]{:S(2)}) collective-permute-start(bf16[2048,256]{1,0:T(8,128)(2,1)} %get-tuple-element.3550), channel_id=1, source_target_pairs={{1,0},{2,1},{3,2},{5,4},{6,5},{7,6},{9,8},{10,9},{11,10},{13,12},{... | collective-permute-start | bytes 3145736 | tf_op jit(solution)/shard_map/ppermute | solution.py:16
  536.0 26.9 %collective-permute-start.5 = (bf16[2048,256]{1,0:T(8,128)(2,1)}, bf16[2048,256]{1,0:T(8,128)(2,1)}, u32[]{:S(2)}, u32[]{:S(2)}) collective-permute-start(bf16[2048,256]{1,0:T(8,128)(2,1)} %get-tuple-element.3552), channel_id=1, source_target_pairs={{1,0},{2,1},{3,2},{5,4},{6,5},{7,6},{9,8},{10,9},{11,10},{13,12},{... | collective-permute-start | bytes 3145736 | tf_op jit(solution)/shard_map/ppermute | solution.py:16
  585.3 331.5 %collective-permute-start.6 = (bf16[2048,256]{1,0:T(8,128)(2,1)}, bf16[2048,256]{1,0:T(8,128)(2,1)S(1)}, u32[]{:S(2)}, u32[]{:S(2)}) collective-permute-start(bf16[2048,256]{1,0:T(8,128)(2,1)} %get-tuple-element.3554), channel_id=1, source_target_pairs={{1,0},{2,1},{3,2},{5,4},{6,5},{7,6},{9,8},{10,9},{11,10},{13,12},{... | collective-permute-start | bytes 3145736 | tf_op jit(solution)/shard_map/ppermute | solution.py:16
  589.6 327.3 %copy-start.87 = (bf16[2,2048,256]{2,1,0:T(8,128)(2,1)S(1)}, bf16[2,2048,256]{2,1,0:T(8,128)(2,1)}, u32[]{:S(2)}) copy-start(bf16[2,2048,256]{2,1,0:T(8,128)(2,1)} %all-gather.5.cloned.1.call-done) | copy-start | bytes 6291460
  602.5 314.5 %copy-start.160 = (bf16[256,512]{1,0:T(8,128)(2,1)S(1)}, bf16[256,512]{1,0:T(8,128)(2,1)}, u32[]{:S(2)}) copy-start(bf16[256,512]{1,0:T(8,128)(2,1)} %dynamic-slice_bitcast_fusion.7) | copy-start | bytes 786436
  602.5 314.5 %copy-start.163 = (f32[1,512]{1,0:T(1,128)S(1)}, f32[1,512]{1,0:T(1,128)}, u32[]{:S(2)}) copy-start(f32[1,512]{1,0:T(1,128)} %copy-done.161) | copy-start | bytes 6148
  1202.9 42.5 %collective-permute-start.7 = (bf16[2048,256]{1,0:T(8,128)(2,1)}, bf16[2048,256]{1,0:T(8,128)(2,1)}, u32[]{:S(2)}, u32[]{:S(2)}) collective-permute-start(bf16[2048,256]{1,0:T(8,128)(2,1)} %get-tuple-element.3556), channel_id=1, source_target_pairs={{1,0},{2,1},{3,2},{5,4},{6,5},{7,6},{9,8},{10,9},{11,10},{13,12},{... | collective-permute-start | bytes 3145736 | tf_op jit(solution)/shard_map/ppermute | solution.py:16
  1551.6 186.6 %reduce-scatter.5.cloned.1.call-start = ((), (), s32[]{:S(2)}) async-start(), calls=%async_computation.5 | async-start | bytes 2621440 | tf_op jit(solution)/shard_map/reduce_scatter | solution.py:449
  (239 other events, 7715.3 us)
Sparse Core Ops, SparseCore 0:
  9.6 48.6 all-gather.2
  59.9 43.5 all-gather.4
  369.6 129.6 reduce-scatter.2
  1551.7 141.1 all-reduce.3
  1695.7 42.4 reduce-scatter.4
where the time goes:
time: 1770 us; the launch traced here: 1750 us
  waiting for transfers between devices  647 us (37%)
  matrix products  433 us (24%)
  other arithmetic  309 us (17%)
  loops' own time  141 us (8%)
  local copies, waits for them, and re-layouts  139 us (8%)
  blocking collectives  38.7 us (2%)
  starting transfers between devices  26.8 us (2%)
    ppermute x8, waiting for transfers between devices, passed_along(): return lax.ppermute(value, axis, pairs)  481 us
    dot_general x16, matrix products, context_one_block(): jnp.einsum('hqk,khd->qhd', weights_low, value_heads, preferred_element_ty...  108 us
    dot_general x8, matrix products, gradient_one_block(): jnp.einsum('qhd,khd->hqk', context_block, value_heads, preferred_element_...  88.4 us
    convert_element_type x8, other arithmetic, gradient_one_block(): score_grads = (weights_full * (weight_grads - inner)).astype(jnp.bfloat16)  87.5 us
    psum x1, waiting for transfers between devices, body(): lax.psum((in_total, in_bias_total, out_total, out_bias_total, attend_gain...  82.9 us
    another operation x5, loops' own time, body(): lax.switch(branch, [back_attend, back_expand, back_spare], kept_inputs[sl...  64.5 us
    dot_general x8, matrix products, gradient_one_block(): jnp.einsum('hqk,qhd->khd', weights_low, context_block, preferred_element_...  60.3 us
    dot_general x16, matrix products, masked_scores(): jnp.einsum('qhd,khd->hqk', query_block, key_heads, preferred_element_type...  58.3 us
  transfers between devices with their start and end apart: 13, of which 11 were waited for; matrix products, arithmetic and copies ran while one was open for 45% of the time, Pallas kernels for 0%

commit v1 on v0

v1 whole, which is shorter than its diff:
```python
from types import SimpleNamespace

import jax
import jax.numpy as jnp
from jax import lax
from jax.experimental import pallas as pl
from jax.experimental.pallas import tpu as pltpu
from jax.sharding import PartitionSpec as P

HEADS = 4
EPSILON = 1e-12
MASKED = -1e30
DOCS = 8
TB = 256
QB = 128
LANES = 128
VMEM_LIMIT = 60 * 1024 * 1024

BF = jnp.bfloat16
F32 = jnp.float32

KEPT = dict(
    x=(256, BF),
    qkv=(768, BF),
    ctx=(256, BF),
    n1=(256, BF),
    r1=(128, F32),
    mid=(256, BF),
    act=(512, BF),
    slope=(512, BF),
    n2=(256, BF),
    r2=(128, F32),
)
NAMES = tuple(KEPT)


def dot(a, b):
    return jnp.dot(a, b, preferred_element_type=F32)


def dot_nt(a, b):
    return lax.dot_general(a, b, (((1,), (1,)), ((), ())), preferred_element_type=F32)


def dot_tn(a, b):
    return lax.dot_general(a, b, (((0,), (0,)), ((), ())), preferred_element_type=F32)


def fold(v):
    return v.reshape(-1, 8, v.shape[-1]).sum(0)


def rows_at(start, count):
    return pl.ds(pl.multiple_of(start, 16), count)


def block(b):
    return pl.ds(pl.multiple_of(b * TB, TB), TB)


class Plan:
    def __init__(self, given, table, items):
        self.given, self.table, self.items = given, table, items

        def one(d, carry):
            offset, tile = carry
            table[d] = offset
            table[items + d] = tile
            length = given[items + d]
            count = lax.shift_right_logical(length + (QB - 1), 7)
            return offset + lax.bitwise_and(length + 15, -16), tile + count * count

        total, _ = lax.fori_loop(0, items, one, (jnp.int32(0), jnp.int32(0)))
        self.blocks = lax.shift_right_logical(total + (TB - 1), 8)

    def start(self, d):
        return self.given[d]

    def length(self, d):
        return self.given[self.items + d]

    def offset(self, d):
        return self.table[d]

    def tile(self, d):
        return self.table[self.items + d]

    def over_docs(self, most, visit):
        def one(d, _):
            length = self.length(d)
            for n in range(1, most + 1):

                @pl.when(lax.shift_right_logical(length + (QB - 1), 7) == n)
                def _():
                    visit(d, n, length)

            return 0

        lax.fori_loop(0, self.items, one, 0)

    def over_blocks(self, visit):
        def one(b, _):
            visit(b)
            return 0

        lax.fori_loop(0, self.blocks, one, 0)


def fill_window(win, own, left, right, span):
    half = left.shape[1]
    whole = own.shape[1]
    for r in range(own.shape[0]):
        base = r * span
        win[pl.ds(base, half), :] = left[r]
        win[pl.ds(base + half, whole), :] = own[r]
        win[pl.ds(base + half + whole, half), :] = right[r]
        clear(win, pl.ds(base + 2 * whole, span - 2 * whole))


REACH = QB + 16


def pack(plan, most, win, dst):
    plan.over_blocks(lambda b: clear(dst, block(b)))

    def visit(d, n, length):
        start, offset = plan.start(d), plan.offset(d)
        shift = lax.bitwise_and(start, 15)
        row = lax.broadcasted_iota(jnp.int32, (QB, REACH), 0)
        col = lax.broadcasted_iota(jnp.int32, (QB, REACH), 1)
        for q in range(n):
            rows = win[rows_at(start - shift + q * QB, REACH), :]
            taken = (col == row + shift) & (row < length - q * QB)
            picked = dot(jnp.where(taken, 1.0, 0.0).astype(BF), rows)
            dst[rows_at(offset + q * QB, QB), :] = picked.astype(BF)

    plan.over_docs(most, visit)


def unpack(plan, most, src, win, own, left, right, span):
    win[...] = jnp.zeros(win.shape, BF)
    clear(src, rows_at(plan.blocks * TB, QB))

    def visit(d, n, length):
        start, offset = plan.start(d), plan.offset(d)
        shift = lax.bitwise_and(start, 15)
        row = lax.broadcasted_iota(jnp.int32, (REACH, QB), 0)
        col = lax.broadcasted_iota(jnp.int32, (REACH, QB), 1)
        for q in range(n):
            rows = src[rows_at(offset + q * QB, QB), :]
            taken = (row == col + shift) & (col < length - q * QB)
            placed = dot(jnp.where(taken, 1.0, 0.0).astype(BF), rows)
            at = rows_at(start - shift + q * QB, REACH)
            win[at, :] = (win[at, :].astype(F32) + placed).astype(BF)

    plan.over_docs(most, visit)
    half = left.shape[1]
    whole = own.shape[1]
    for r in range(own.shape[0]):
        base = r * span
        left[r] = win[pl.ds(base, half), :]
        own[r] = win[pl.ds(base + half, whole), :]
        right[r] = win[pl.ds(base + half + whole, half), :]


def clear(ref, rows):
    ref[rows, :] = jnp.zeros((rows.size, ref.shape[1]), ref.dtype)


def head_masks():
    lane = lax.broadcasted_iota(jnp.int32, (1, LANES), 1)
    low = (lane < LANES // 2).astype(F32)
    return low.astype(BF), (1.0 - low).astype(BF)


def two_heads(v, masks):
    return jnp.concatenate([v * masks[0], v * masks[1]], axis=0)


def one_of_two(v):
    lane = lax.broadcasted_iota(jnp.int32, (QB, LANES), 1)
    return jnp.where(lane < LANES // 2, v[:QB], v[QB:])


def project(plan, kept, weight, bias):
    scaling = (weight.shape[0] // HEADS) ** (-0.5)

    def visit(b):
        rows = block(b)
        y = dot(kept.x[rows, :], weight[...])
        queries = (y[:, 0:256] + bias[:, 0:256]).astype(BF)
        kept.qkv[rows, 0:256] = queries * jnp.asarray(scaling, BF)
        kept.qkv[rows, 256:512] = y[:, 256:512].astype(BF)
        kept.qkv[rows, 512:768] = (y[:, 512:768] + bias[:, 256:512]).astype(BF)
        clear(kept.ctx, rows)

    plan.over_blocks(visit)
    clear(kept.qkv, rows_at(plan.blocks * TB, QB))


def attend(plan, most, kept, weights_low):
    masks = head_masks()

    def visit(d, n, length):
        offset, tile = plan.offset(d), plan.tile(d)
        width = n * QB
        keys_at = rows_at(offset, width)

        def one(q, _):
            queries_at = rows_at(offset + q * QB, QB)
            row = lax.broadcasted_iota(jnp.int32, (QB, 1), 0) + q * QB
            row = jnp.concatenate([row, row], axis=0)
            for g in range(2):
                cols = g * LANES
                keys = kept.qkv[keys_at, 256 + cols : 256 + cols + LANES]
                values = kept.qkv[keys_at, 512 + cols : 512 + cols + LANES]
                queries = two_heads(kept.qkv[queries_at, cols : cols + LANES], masks)
                scores = dot_nt(queries, keys)
                last = scores[:, width - QB :]
                col = lax.broadcasted_iota(jnp.int32, last.shape, 1)
                last = jnp.where(col < length - (width - QB), last, MASKED)
                if n > 1:
                    scores = jnp.concatenate([scores[:, : width - QB], last], axis=1)
                else:
                    scores = last
                highest = jnp.max(scores, axis=1, keepdims=True)
                raised = jnp.exp(scores - highest)
                total = jnp.sum(raised, axis=1, keepdims=True)
                share = jnp.where(row < length, 1.0 / total, 0.0)
                probs = (raised * share).astype(BF)
                for k in range(n):
                    weights_low[tile + q * n + k, g] = probs[:, k * QB : (k + 1) * QB]
                context = one_of_two(dot(probs, values))
                kept.ctx[queries_at, cols : cols + LANES] = context.astype(BF)
            return 0

        lax.fori_loop(0, n, one, 0)

    plan.over_docs(most, visit)


def normal(v):
    centred = v - jnp.mean(v, axis=1, keepdims=True)
    spread = jnp.mean(centred * centred, axis=1, keepdims=True)
    rate = lax.rsqrt(spread + EPSILON)
    return centred * rate, rate


def feed(plan, kept, w, out, each=None):
    def visit(b):
        rows = block(b)
        x = kept.x[rows, :].astype(F32)
        attn_sum = x + dot(kept.ctx[rows, :], w.wout[...]) + w.bout[...]
        n1, r1 = normal(attn_sum)
        kept.n1[rows, :] = n1.astype(BF)
        kept.r1[rows, :] = jnp.broadcast_to(r1, (TB, LANES))
        mid_low = (n1 * w.g1[...] + w.s1[...]).astype(BF)
        kept.mid[rows, :] = mid_low
        pre_up = dot(mid_low, w.wup[...]) + w.bup[...]
        share = 0.5 + 0.5 * lax.erf(pre_up * (0.5**0.5))
        density = jnp.exp(pre_up * pre_up * -0.5) * 0.3989422804014327
        active = (pre_up * share).astype(BF)
        kept.act[rows, :] = active
        kept.slope[rows, :] = (share + pre_up * density).astype(BF)
        feed_sum = mid_low.astype(F32) + dot(active, w.wdown[...]) + w.bdown[...]
        n2, r2 = normal(feed_sum)
        kept.n2[rows, :] = n2.astype(BF)
        kept.r2[rows, :] = jnp.broadcast_to(r2, (TB, LANES))
        out[rows, :] = (n2 * w.g2[...] + w.s2[...]).astype(BF)
        if each is not None:
            each(b)

    plan.over_blocks(visit)


AT_OUT, AT_UP, AT_DOWN, AT_ALL = 768, 1024, 1536, 2048
V_IN, V_OUT, V_G1, V_S1, V_UP, V_DOWN, V_G2, V_S2, V_ALL = 0, 2, 3, 4, 5, 7, 8, 9, 16


def norm_back(upstream, n, rate, gain):
    e = upstream * gain
    inner = jnp.mean(e * n, axis=1, keepdims=True)
    return (e - jnp.mean(e, axis=1, keepdims=True) - n * inner) * rate


def feed_back(plan, kept, w, upstream, r):
    total, small, ctx_grad, sum_grad = r.s_total, r.s_small, r.s_ctx_grad, r.s_sum_grad

    def visit(b):
        rows = block(b)
        up = upstream[rows, :].astype(F32)
        n2 = kept.n2[rows, :].astype(F32)
        small[V_G2] += fold(up * n2)
        small[V_S2] += fold(up)
        r2 = kept.r2[rows, :]
        feed_grad = norm_back(up, n2, jnp.concatenate([r2, r2], axis=1), w.g2[...])
        low = feed_grad.astype(BF)
        small[V_DOWN] += fold(low.astype(F32))
        total[AT_DOWN:AT_ALL, :] += dot_tn(kept.act[rows, :], low)
        active_grad = dot_nt(low, w.wdown[...])
        pre_grad = (active_grad * kept.slope[rows, :].astype(F32)).astype(BF)
        sums = fold(pre_grad.astype(F32))
        small[V_UP] += sums[:, :256]
        small[V_UP + 1] += sums[:, 256:]
        up_grad = dot_tn(kept.mid[rows, :], pre_grad)
        total[AT_UP : AT_UP + 256, :] += up_grad[:, :256]
        total[AT_UP + 256 : AT_DOWN, :] += up_grad[:, 256:]
        mid_grad = (dot_nt(pre_grad, w.wup[...]) + feed_grad).astype(BF).astype(F32)
        n1 = kept.n1[rows, :].astype(F32)
        small[V_G1] += fold(mid_grad * n1)
        small[V_S1] += fold(mid_grad)
        r1 = kept.r1[rows, :]
        attn_grad = norm_back(mid_grad, n1, jnp.concatenate([r1, r1], axis=1), w.g1[...])
        sum_grad[rows, :] = attn_grad
        low = attn_grad.astype(BF)
        small[V_OUT] += fold(low.astype(F32))
        total[AT_OUT:AT_UP, :] += dot_tn(kept.ctx[rows, :], low)
        ctx_grad[rows, :] = dot_nt(low, w.wout[...]).astype(BF)

    plan.over_blocks(visit)
    clear(ctx_grad, rows_at(plan.blocks * TB, QB))


def attend_back(plan, most, kept, r):
    weights_low, ctx_grad, qkv_grad = r.s_probs, r.s_ctx_grad, r.s_qkv_grad
    key_sums, value_sums = r.s_key_sums, r.s_value_sums
    masks = head_masks()
    scaling = (256 // HEADS) ** (-0.5)
    plan.over_blocks(lambda b: clear(qkv_grad, block(b)))

    def visit(d, n, length):
        offset, tile = plan.offset(d), plan.tile(d)
        width = n * QB
        keys_at = rows_at(offset, width)
        key_sums[:width, :] = jnp.zeros((width, 256), F32)
        value_sums[:width, :] = jnp.zeros((width, 256), F32)

        def one(q, _):
            queries_at = rows_at(offset + q * QB, QB)
            for g in range(2):
                cols = g * LANES
                here = slice(cols, cols + LANES)
                keys = kept.qkv[keys_at, 256 + cols : 256 + cols + LANES]
                values = kept.qkv[keys_at, 512 + cols : 512 + cols + LANES]
                queries = two_heads(kept.qkv[queries_at, here], masks)
                grads = two_heads(ctx_grad[queries_at, here], masks)
                probs = [weights_low[tile + q * n + k, g] for k in range(n)]
                probs = jnp.concatenate(probs, axis=1) if n > 1 else probs[0]
                full = probs.astype(F32)
                prob_grad = dot_nt(grads, values)
                inner = jnp.sum(full * prob_grad, axis=1, keepdims=True)
                score_grad = (full * (prob_grad - inner)).astype(BF)
                query_grad = one_of_two(dot(score_grad, keys)) * scaling
                qkv_grad[queries_at, here] = query_grad.astype(BF)
                key_sums[:width, here] += dot_tn(score_grad, queries)
                value_sums[:width, here] += dot_tn(probs, grads)
            return 0

        lax.fori_loop(0, n, one, 0)
        qkv_grad[keys_at, 256:512] = key_sums[:width, :].astype(BF)
        qkv_grad[keys_at, 512:768] = value_sums[:width, :].astype(BF)

    plan.over_docs(most, visit)


def project_back(plan, kept, w, r, out):
    qkv_grad, sum_grad, total, small = r.s_qkv_grad, r.s_sum_grad, r.s_total, r.s_small

    def visit(b):
        rows = block(b)
        grad = qkv_grad[rows, :]
        sums = fold(grad.astype(F32))
        small[V_IN] += sums[:, :256]
        small[V_IN + 1] += sums[:, 512:]
        in_grad = dot_tn(kept.x[rows, :], grad)
        for k in range(3):
            total[256 * k : 256 * (k + 1), :] += in_grad[:, 256 * k : 256 * (k + 1)]
        hidden_grad = dot_nt(grad, w.win[...]) + sum_grad[rows, :]
        out[rows, :] = hidden_grad.astype(BF)

    plan.over_blocks(visit)


def first_kernel(layer, most, span, items, r):
    plan = Plan(r.plan, r.s_table, items)
    kept = SimpleNamespace(**{k: getattr(r, "s_" + k) for k in NAMES})
    w = layer_of(r, layer)

    def copy_block(k, b):
        there = getattr(r, "o_" + k).at[block(b)]
        return pltpu.make_async_copy(getattr(kept, k).at[block(b)], there, r.sems.at[NAMES.index(k)])

    def copy_probs(d, n):
        at = pl.ds(plan.tile(d), n * n)
        return pltpu.make_async_copy(r.s_probs.at[at], r.o_probs.at[at], r.sems.at[len(NAMES)])

    fill_window(r.s_window, r.own, r.left, r.right, span)
    pack(plan, most, r.s_window, kept.x)
    project(plan, kept, w.win, w.bin)
    early, late = NAMES[:2], NAMES[2:]
    plan.over_blocks(lambda b: [copy_block(k, b).start() for k in early])
    attend(plan, most, kept, r.s_probs)
    plan.over_docs(most, lambda d, n, length: copy_probs(d, n).start())
    feed(plan, kept, w, r.o_next, lambda b: [copy_block(k, b).start() for k in late])
    plan.over_blocks(lambda b: [copy_block(k, b).wait() for k in NAMES])
    plan.over_docs(most, lambda d, n, length: copy_probs(d, n).wait())


def second_kernel(layer, most, span, items, r):
    plan = Plan(r.plan, r.s_table, items)
    kept = SimpleNamespace(**{k: getattr(r, "s_" + k) for k in NAMES[1:]}, x=r.x)
    w = layer_of(r, layer)
    project(plan, kept, w.win, w.bin)
    attend(plan, most, kept, r.s_probs)
    feed(plan, kept, w, r.s_rows)
    unpack(plan, most, r.s_rows, r.s_window, r.o_own, r.o_left, r.o_right, span)
    fill_window(r.s_window, r.own, r.left, r.right, span)
    pack(plan, most, r.s_window, r.s_rows)
    clear_totals(r)
    feed_back(plan, kept, w, r.s_rows, r)
    attend_back(plan, most, kept, r)
    project_back(plan, kept, w, r, r.o_next)
    send_pieces(r)
    r.o_small[...] = r.s_small[...].sum(1)


def third_kernel(layer, most, span, items, r):
    plan = Plan(r.plan, r.s_table, items)
    kept = SimpleNamespace(**{k: getattr(r, "s_" + k) for k in NAMES})
    w = layer_of(r, layer)

    def copy_block(k, b):
        given = getattr(r, "i_" + k).at[block(b)]
        return pltpu.make_async_copy(given, getattr(kept, k).at[block(b)], r.sems.at[NAMES.index(k)])

    def copy_probs(d, n):
        at = pl.ds(plan.tile(d), n * n)
        return pltpu.make_async_copy(r.i_probs.at[at], r.s_probs.at[at], r.sems.at[len(NAMES)])

    early, late = NAMES[2:], NAMES[:2]
    plan.over_blocks(lambda b: [copy_block(k, b).start() for k in early])
    plan.over_docs(most, lambda d, n, length: copy_probs(d, n).start())
    plan.over_blocks(lambda b: [copy_block(k, b).start() for k in late])
    clear_totals(r)
    plan.over_blocks(lambda b: [copy_block(k, b).wait() for k in early])
    feed_back(plan, kept, w, r.rows, r)
    plan.over_docs(most, lambda d, n, length: copy_probs(d, n).wait())
    plan.over_blocks(lambda b: [copy_block(k, b).wait() for k in late])
    clear(kept.qkv, rows_at(plan.blocks * TB, QB))
    attend_back(plan, most, kept, r)
    project_back(plan, kept, w, r, r.s_rows)
    unpack(plan, most, r.s_rows, r.s_window, r.o_own, r.o_left, r.o_right, span)
    send_pieces(r)
    send_small(r)


def layer_of(r, layer):
    w = SimpleNamespace(win=r.win, wout=r.wout, wup=r.wup, wdown=r.wdown)
    w = SimpleNamespace(**{k: v.at[layer] for k, v in vars(w).items()})
    vectors = dict(bin=r.bin, bout=r.bout, g1=r.g1, s1=r.s1, bup=r.bup, bdown=r.bdown, g2=r.g2, s2=r.s2)
    return SimpleNamespace(**vars(w), **{k: v[layer : layer + 1, :] for k, v in vectors.items()})


def clear_totals(r):
    r.s_total[...] = jnp.zeros(r.s_total.shape, F32)
    r.s_small[...] = jnp.zeros(r.s_small.shape, F32)


def send_pieces(r):
    count = 2 * r.o_keep.shape[0]
    rows = AT_ALL // count
    for p in range(count):
        out = r.o_keep if p < count // 2 else r.o_send
        piece = lax.bitwise_xor(jnp.int32(p), r.self[0])
        at = pl.ds(pl.multiple_of(piece * rows, rows), rows)
        out[p % (count // 2), 0:rows, :] = r.s_total[at, :].astype(BF)


def send_small(r):
    count = 2 * r.o_keep.shape[0]
    rows = AT_ALL // count
    extra = r.o_keep.shape[1] - rows
    share = 2 * V_ALL // count
    r.s_both[0:V_ALL, :] = r.s_small[...].sum(1)
    r.s_both[V_ALL : 2 * V_ALL, :] = r.small[...]
    for j in range(count):
        own = r.s_both[j * share : (j + 1) * share, :]
        r.s_spread[j] = jnp.concatenate([own, jnp.zeros((extra - share, own.shape[1]), F32)], axis=0)
    for p in range(count):
        out = r.o_keep if p < count // 2 else r.o_send
        piece = lax.bitwise_xor(jnp.int32(p), r.self[0])
        out[p % (count // 2), rows : rows + extra, :] = r.s_spread[piece].astype(BF)


def last_kernel(r):
    half = r.keep0.shape[0]
    count = 2 * half
    rows = AT_ALL // count
    share = 2 * V_ALL // count
    for layer, (keep, got) in enumerate(((r.keep0, r.got0), (r.keep1, r.got1))):
        for p in range(count):
            piece = lax.bitwise_xor(jnp.int32(p), r.self[layer])
            source = keep if p < half else got
            r.s_pieces[layer, piece, 0 : keep.shape[1], :] = source[p % half]
    for layer in range(2):
        for j in range(count):
            value = r.s_pieces[layer, j, 0:rows, :].astype(F32)
            at = j * rows
            for low, high, out in (
                (0, AT_OUT, r.o_in),
                (AT_OUT, AT_UP, r.o_out),
                (AT_UP, AT_DOWN, r.o_up),
                (AT_DOWN, AT_ALL, r.o_down),
            ):
                if low <= at < high:
                    tall = out.shape[1]
                    line, col = (at - low) % tall, (at - low) // tall * 256
                    out[layer, line : line + rows, col : col + 256] = value
    for j in range(count):
        tail = r.s_pieces[0, j, rows : rows + 16, :].astype(F32)
        r.s_both[j * share : (j + 1) * share, :] = tail[0:share]
    for layer in range(2):
        at = layer * V_ALL
        here = pl.ds(layer, 1)

        def line(k):
            return r.s_both[at + k : at + k + 1, :]

        r.o_bin[here, :] = jnp.concatenate([line(V_IN), line(V_IN + 1)], axis=1)
        r.o_bout[here, :] = line(V_OUT)
        r.o_g1[here, :] = line(V_G1)
        r.o_s1[here, :] = line(V_S1)
        r.o_bup[here, :] = jnp.concatenate([line(V_UP), line(V_UP + 1)], axis=1)
        r.o_bdown[here, :] = line(V_DOWN)
        r.o_g2[here, :] = line(V_G2)
        r.o_s2[here, :] = line(V_S2)


def call(kernel, consts, inputs, outputs, scratch, flops):
    names = tuple(inputs) + tuple(outputs) + tuple(scratch)

    def run(*refs):
        kernel(*consts, SimpleNamespace(**dict(zip(names, refs))))

    got = pl.pallas_call(
        run,
        out_shape=[jax.ShapeDtypeStruct(s, d) for s, d, _ in outputs.values()],
        in_specs=[spec for _, spec in inputs.values()],
        out_specs=[spec for _, _, spec in outputs.values()],
        scratch_shapes=list(scratch.values()),
        compiler_params=pltpu.CompilerParams(vmem_limit_bytes=VMEM_LIMIT),
        cost_estimate=pl.CostEstimate(flops=flops, bytes_accessed=8 << 20, transcendentals=0),
    )(*[a for a, _ in inputs.values()])
    return SimpleNamespace(**dict(zip(outputs, got)))


def make_plan(segments, place, section_count):
    row_count, length = segments.shape
    whole = length // section_count
    half = whole // 2
    span = 2 * whole + 2 * QB
    ids = jnp.arange(DOCS + 1, dtype=jnp.int32)
    starts = jnp.sum((segments[:, None, :] < ids[None, :, None]).astype(jnp.int32), axis=2)
    targets = jnp.arange(1, section_count, dtype=jnp.int32) * whole
    away = starts[None] - targets[:, None, None]
    far = (jnp.abs(away) > half).astype(jnp.int32) * (1 << 16)
    base = DOCS + 1
    if row_count == 2:
        cost = jnp.abs(away[:, 0, :, None] + away[:, 1, None, :])
        cost = cost + far[:, 0, :, None] + far[:, 1, None, :]
        code = ids[:, None] * base + ids[None, :]
        best = jnp.min(cost * (base * base) + code[None], axis=(1, 2)) % (base * base)
        chosen = jnp.stack([best // base, best % base], axis=1)
    else:
        chosen = jnp.min((jnp.abs(away) + far) * base + ids, axis=2) % base
    first = jnp.zeros((1, row_count), jnp.int32)
    cuts = jnp.concatenate([first, chosen, first + DOCS], axis=0)
    sections = jnp.arange(section_count + 1)[:, None]
    low = jnp.sum(jnp.where(sections == place, cuts, 0), axis=0)[:, None]
    high = jnp.sum(jnp.where(sections == place + 1, cuts, 0), axis=0)[:, None]
    here = (ids[None, :DOCS] >= low) & (ids[None, :DOCS] < high)
    lengths = jnp.where(here, starts[:, 1:] - starts[:, :-1], 0)
    begins = starts[:, :-1] - place * whole + half
    begins = begins + jnp.arange(row_count, dtype=jnp.int32)[:, None] * span
    begins = jnp.where(here, begins, 0)
    return jnp.stack([begins, lengths]).reshape(-1)


def swapped(low_part, high_part, place, odd):
    count = lax.axis_size("pipe")
    pairs = [(i, i + 1) for i in range(odd, count - 1, 2)]
    upper = lax.rem(place + odd, 2) == 1
    sent = jnp.where(upper, low_part, high_part)
    got = lax.ppermute(sent, "pipe", [p for i, j in pairs for p in ((i, j), (j, i))])
    return upper, got


def halo(low_part, high_part, place):
    even_upper, even = swapped(low_part, high_part, place, 0)
    odd_upper, odd = swapped(low_part, high_part, place, 1)
    return jnp.where(even_upper, even, odd), jnp.where(odd_upper, even, odd)


def orders():
    found = []
    for axis in ("dp", "pipe"):
        stride = 1
        while stride < lax.axis_size(axis):
            found.append((axis, stride))
            stride *= 2
    other = list(found)
    if len(found) > 2:
        other[1], other[2] = found[2], found[1]
    return found, other


SPLIT = 4


def self_index(order):
    index = jnp.int32(0)
    for axis, stride in order[:SPLIT]:
        index = 2 * index + lax.rem(lax.div(lax.axis_index(axis), stride), 2)
    return index.astype(jnp.int32)


def exchange(value, axis, stride):
    count = lax.axis_size(axis)
    return lax.ppermute(value, axis, [(i, i ^ stride) for i in range(count)])


def added(a, b):
    return (a.astype(F32) + b.astype(F32)).astype(BF)


def sum_steps(keep, send, order):
    total = None
    for k, (axis, stride) in enumerate(order[:SPLIT]):
        got = exchange(send, axis, stride)
        yield None
        half = keep.shape[0] // 2
        if half:
            send, keep = added(keep[half:], got[half:]), added(keep[:half], got[:half])
        else:
            total = added(keep, got)
    for axis, stride in order[SPLIT:]:
        got = exchange(total, axis, stride)
        yield None
        total = added(total, got)
    for k, (axis, stride) in enumerate(reversed(order[:SPLIT])):
        got = exchange(total, axis, stride)
        yield (total, got)
        total = jnp.concatenate([total, got], axis=0)


def body(
    tokens,
    segments,
    cotangent,
    attention_in,
    attention_in_bias,
    attention_out,
    attention_out_bias,
    attention_gain,
    attention_shift,
    expand_weight,
    expand_bias,
    contract_weight,
    contract_bias,
    feed_gain,
    feed_shift,
):
    section_count = lax.axis_size("pipe")
    place = lax.axis_index("pipe").astype(jnp.int32)
    row_count, whole, features = tokens.shape
    half = whole // 2
    span = 2 * whole + 2 * QB
    items = row_count * DOCS
    most = whole // QB
    cap = row_count * 2 * whole + items * 16 + QB
    cap = (cap + TB - 1) // TB * TB
    tiles = row_count * 42
    vmem = pl.BlockSpec(memory_space=pltpu.VMEM)
    smem = pl.BlockSpec(memory_space=pltpu.SMEM)
    anywhere = pl.BlockSpec(memory_space=pl.ANY)
    weights = dict(
        win=attention_in,
        bin=attention_in_bias,
        wout=attention_out,
        bout=attention_out_bias,
        g1=attention_gain,
        s1=attention_shift,
        wup=expand_weight,
        bup=expand_bias,
        wdown=contract_weight,
        bdown=contract_bias,
        g2=feed_gain,
        s2=feed_shift,
    )
    weights = {k: (v, vmem) for k, v in weights.items()}

    def with_halo(value):
        left, right = halo(value[:, :half], value[:, half:], place)
        return dict(own=(value, vmem), left=(left, vmem), right=(right, vmem))

    def placed(got):
        low, high = halo(got.o_left, got.o_right, place)
        return got.o_own + jnp.concatenate([low, high], axis=1)

    order0, order1 = orders()
    selves = [self_index(order0), self_index(order1)]
    pieces = 1 << SPLIT
    token_rows = with_halo(tokens)
    plan = dict(plan=(make_plan(segments, place, section_count), smem))
    kept_scratch = {"s_" + k: pltpu.VMEM((cap, c), t) for k, (c, t) in KEPT.items()}
    probs_shape = (tiles, 2, 2 * QB, QB)
    kept_scratch.update(
        s_probs=pltpu.VMEM(probs_shape, BF),
        s_window=pltpu.VMEM((row_count * span, features), BF),
        s_table=pltpu.SMEM((2 * items,), jnp.int32),
    )
    sems = dict(sems=pltpu.SemaphoreType.DMA((len(NAMES) + 1,)))
    back_scratch = dict(
        s_rows=pltpu.VMEM((cap, features), BF),
        s_total=pltpu.VMEM((AT_ALL, features), F32),
        s_small=pltpu.VMEM((V_ALL, 8, features), F32),
        s_ctx_grad=pltpu.VMEM((cap, features), BF),
        s_sum_grad=pltpu.VMEM((cap, features), F32),
        s_qkv_grad=pltpu.VMEM((cap, 3 * features), BF),
        s_key_sums=pltpu.VMEM((whole, features), F32),
        s_value_sums=pltpu.VMEM((whole, features), F32),
    )
    window_out = dict(
        o_own=((row_count, whole, features), BF, vmem),
        o_left=((row_count, half, features), BF, vmem),
        o_right=((row_count, half, features), BF, vmem),
    )

    def pieces_out(extra):
        shape = (pieces // 2, AT_ALL // pieces + extra, features)
        return dict(o_keep=(shape, BF, vmem), o_send=(shape, BF, vmem))

    next_out = dict(o_next=((cap, features), BF, vmem))
    kept_out = {"o_" + k: ((cap, c), t, anywhere) for k, (c, t) in KEPT.items()}
    kept_out.update(o_probs=(probs_shape, BF, anywhere))

    first = call(
        first_kernel,
        (0, most, span, items),
        plan | token_rows | weights,
        kept_out | next_out,
        kept_scratch | sems,
        12 << 30,
    )
    cotangent_rows = with_halo(cotangent)
    second = call(
        second_kernel,
        (1, most, span, items),
        plan
        | cotangent_rows
        | dict(x=(first.o_next, vmem), self=(selves[1].reshape(1), smem))
        | weights,
        window_out
        | pieces_out(0)
        | next_out
        | dict(o_small=((V_ALL, features), F32, vmem)),
        {k: v for k, v in kept_scratch.items() if k != "s_x"} | back_scratch,
        36 << 30,
    )
    kept_in = {"i_" + k: (getattr(first, "o_" + k), anywhere) for k in NAMES + ("probs",)}
    third = call(
        third_kernel,
        (0, most, span, items),
        plan
        | kept_in
        | dict(
            rows=(second.o_next, vmem),
            small=(second.o_small, vmem),
            self=(selves[0].reshape(1), smem),
        )
        | weights,
        window_out | pieces_out(16),
        kept_scratch
        | back_scratch
        | sems
        | dict(
            s_both=pltpu.VMEM((2 * V_ALL, features), F32),
            s_spread=pltpu.VMEM((pieces, 16, features), F32),
        ),
        24 << 30,
    )
    layer_output = placed(second)
    input_grad = placed(third)
    sums = [sum_steps(third.o_keep, third.o_send, order0)]
    sums.append(sum_steps(second.o_keep, second.o_send, order1))
    for ends in zip(*sums):
        pass
    layers = attention_in.shape[0]

    def out(*shape):
        return ((layers,) + shape, F32, vmem)

    vector = out(features)
    result = call(
        last_kernel,
        (),
        dict(
            self=(jnp.stack(selves), smem),
            keep0=(ends[0][0], vmem),
            got0=(ends[0][1], vmem),
            keep1=(ends[1][0], vmem),
            got1=(ends[1][1], vmem),
        ),
        dict(
            o_in=out(features, 3 * features),
            o_bin=out(2 * features),
            o_out=out(features, features),
            o_bout=vector,
            o_g1=vector,
            o_s1=vector,
            o_up=out(features, 2 * features),
            o_bup=out(2 * features),
            o_down=out(2 * features, features),
            o_bdown=vector,
            o_g2=vector,
            o_s2=vector,
        ),
        dict(
            s_pieces=pltpu.VMEM((2, pieces, AT_ALL // pieces + 16, features), BF),
            s_both=pltpu.VMEM((2 * V_ALL, features), F32),
        ),
        1 << 30,
    )
    return (layer_output, input_grad) + tuple(vars(result).values())


def solution(mesh):
    rows = P("dp", "pipe", None)
    return jax.shard_map(
        body,
        mesh=mesh,
        in_specs=(rows, P("dp", None), rows) + (P(),) * 12,
        out_specs=(rows, rows) + (P(),) * 12,
        check_vma=False,
    )
```

time: 1770 us -> 183 us (0.10)
  waiting for transfers between devices: 647 us -> 28.6 us
  matrix products: 433 us -> 0 us
  other arithmetic: 309 us -> 7.24 us
  loops' own time: 141 us -> 0 us
  local copies, waits for them, and re-layouts: 139 us -> 3.16 us
  Pallas kernels: 0 us -> 97.2 us
  blocking collectives: 38.7 us -> 0 us
    ppermute x8 -> x26, waiting for transfers between devices: 481 us -> 28.6 us  [the longest x18 24.7 us: exchange(): return lax.ppermute(value, axis, [(i, i ^ stride) for i in range(count)])]
    dot_general x80 -> x0, matrix products: 433 us -> none  [the longest x16 108 us: context_one_block(): jnp.einsum('hqk,khd->qhd', weights_low, value_heads, preferred_element_ty...]
    another operation x16 -> x0, loops' own time: 141 us -> none  [the longest x5 64.5 us: body(): lax.switch(branch, [back_attend, back_expand, back_spare], kept_inputs[sl...]
    pallas_call x0 -> x4, Pallas kernels: none -> 97.2 us  [call(): pl.pallas_call(run, out_shape=[jax.ShapeDtypeStruct(s, d) for s, d, _ in...]
    convert_element_type x10, other arithmetic: 90.8 us -> 0.55 us  [added(): return (a.astype(F32) + b.astype(F32)).astype(BF)]
    psum x1 -> x0, waiting for transfers between devices: 82.9 us -> none  [body(): lax.psum((in_total, in_bias_total, out_total, out_bias_total, attend_gain...]
    scatter-add x20 -> x0, other arithmetic: 49.4 us -> none  [accumulate_layer(): running_total.at[layer_position].add(summand_term)]
    dynamic_slice x89 -> x0, local copies, waits for them, and re-layouts: 47.6 us -> none  [the longest x16 22.9 us: keep_slot(): stored[slot_index]]
  transfers between devices with their start and end apart: 13 -> 26, of which waited for: 11 -> 13; matrix products, arithmetic and copies ran while one was open for 45% -> 4% of each run, Pallas kernels for 0% -> 28%
where the time goes in v1:
time: 183 us; the launch traced here: 180 us
  Pallas kernels  97.2 us (53%)
  starting transfers between devices  43.1 us (24%)
  waiting for transfers between devices  28.6 us (16%)
  other arithmetic  7.24 us (4%)
  local copies, waits for them, and re-layouts  3.16 us (2%)
    pallas_call x4, Pallas kernels, call(): pl.pallas_call(run, out_shape=[jax.ShapeDtypeStruct(s, d) for s, d, _ in...  97.2 us
    ppermute x18, starting transfers between devices, exchange(): return lax.ppermute(value, axis, [(i, i ^ stride) for i in range(count)])  32.2 us
    ppermute x18, waiting for transfers between devices, exchange(): return lax.ppermute(value, axis, [(i, i ^ stride) for i in range(count)])  24.7 us
    ppermute x8, starting transfers between devices, swapped(): lax.ppermute(sent, 'pipe', [p for i, j in pairs for p in ((i, j), (j, i))])  10.9 us
    ppermute x8, waiting for transfers between devices, swapped(): lax.ppermute(sent, 'pipe', [p for i, j in pairs for p in ((i, j), (j, i))])  3.91 us
  transfers between devices with their start and end apart: 26, of which 13 were waited for; matrix products, arithmetic and copies ran while one was open for 4% of the time, Pallas kernels for 28%

profile of v1, /device:TPU:0, one launch (start us, length us, event | category | flops | bytes accessed | tf_op | source)
XLA Modules:
  0.0 180.5 jit_solution(2493728151477502118)
XLA Ops:
  0.7 1.1 broadcast_select_fusion.7
  1.8 3.1 %collective-permute-start = (bf16[2,256,256]{2,1,0:T(8,128)(2,1)S(1)}, bf16[2,256,256]{2,1,0:T(8,128)(2,1)S(1)}, u32[]{:S(2)}, u32[]{:S(2)}) collective-permute-start(bf16[2,256,256]{2,1,0:T(8,128)(2,1)S(1)} %get-tuple-element.111), channel_id=1, source_target_pairs={{0,1},{1,0},{2,3},{3,2},{4,5},{5,4},{6,7},{7,6},{8,9},{9,8},{10,11... | collective-permute-start | bytes 786440 | tf_op jit(solution)/shard_map/ppermute | solution.py:594
  5.6 4.4 %collective-permute-start.2 = (bf16[2,256,256]{2,1,0:T(8,128)(2,1)S(1)}, bf16[2,256,256]{2,1,0:T(8,128)(2,1)S(1)}, u32[]{:S(2)}, u32[]{:S(2)}) collective-permute-start(bf16[2,256,256]{2,1,0:T(8,128)(2,1)S(1)} %get-tuple-element.107), channel_id=1, source_target_pairs={{0,1},{1,0},{2,3},{3,2},{4,5},{5,4},{6,7},{7,6},{8,9},{9,8},{10,11... | collective-permute-start | bytes 786440 | tf_op jit(solution)/shard_map/ppermute | solution.py:594
  12.9 3.9 %collective-permute-done.2 = bf16[2,256,256]{2,1,0:T(8,128)(2,1)S(1)} collective-permute-done((bf16[2,256,256]{2,1,0:T(8,128)(2,1)S(1)}, bf16[2,256,256]{2,1,0:T(8,128)(2,1)S(1)}, u32[]{:S(2)}, u32[]{:S(2)}) %collective-permute-start.2) | collective-permute-done | bytes 262176 | tf_op jit(solution)/shard_map/ppermute | solution.py:594
  17.6 23.7 %shard_map.254 = (bf16[2560,256]{1,0:T(8,128)(2,1)}, bf16[2560,768]{1,0:T(8,128)(2,1)}, bf16[2560,256]{1,0:T(8,128)(2,1)}, bf16[2560,256]{1,0:T(8,128)(2,1)}, f3...) custom-call(s32[32]{0:T(128)} %reshape.152.refs_0_, ...), custom_call_target="tpu_custom_call" | custom-call | flops 12884901888 | bytes 8388608 | tf_op jit(solution)/shard_map/pallas_call | solution.py:545
  42.2 43.4 %shard_map.255 = (bf16[2,512,256]{2,1,0:T(8,128)(2,1)}, bf16[2,256,256]{2,1,0:T(8,128)(2,1)}, bf16[2,256,256]{2,1,0:T(8,128)(2,1)}, bf16[8,128,256]{2,1,0:T(8,12...) custom-call(s32[32]{0:T(128)} %reshape.152.refs_0_, ...), custom_call_target="tpu_custom_call" | custom-call | flops 38654705664 | bytes 8388608 | tf_op jit(solution)/shard_map/pallas_call | solution.py:545
  85.7 26.2 %shard_map.256 = (bf16[2,512,256]{2,1,0:T(8,128)(2,1)}, bf16[2,256,256]{2,1,0:T(8,128)(2,1)}, bf16[2,256,256]{2,1,0:T(8,128)(2,1)}, bf16[8,144,256]{2,1,0:T(8,128)(2,1)}, bf16[8,144,256]{2,1,0:T(8,128)(2,1)}) custom-call(s32[32]{0:T(128)} %reshape.152.refs_0_, bf16[2560,256]{1,0:T(8,128)(2,1)} %get-tuple-element.54.refs_1_, ...), custom_call_target="tpu_custom_call" | custom-call | flops 25769803776 | bytes 8388608 | tf_op jit(solution)/shard_map/pallas_call | solution.py:545
  112.8 1.9 %collective-permute-start.18 = (bf16[4,128,256]{2,1,0:T(8,128)(2,1)S(1)}, bf16[4,128,256]{2,1,0:T(8,128)(2,1)S(1)}, u32[]{:S(2)}, u32[]{:S(2)}) collective-permute-start(bf16[4,128,256]{2,1,0:T(8,128)(2,1)S(1)} %get-tuple-element.91), channel_id=1, source_target_pairs={{0,16},{4,20},{8,24},{12,28},{16,0},{20,4},{24,8},{28,12},{1,17},{... | collective-permute-start | bytes 786440 | tf_op jit(solution)/shard_map/ppermute | solution.py:629
  114.8 15.5 %collective-permute-start.9 = (bf16[4,144,256]{2,1,0:T(8,128)(2,1)S(1)}, bf16[4,144,256]{2,1,0:T(8,128)(2,1)S(1)}, u32[]{:S(2)}, u32[]{:S(2)}) collective-permute-start(bf16[4,144,256]{2,1,0:T(8,128)(2,1)S(1)} %get-tuple-element.89), channel_id=1, source_target_pairs={{0,8},{4,12},{8,0},{12,4},{16,24},{20,28},{24,16},{28,20},{1,9},{5... | collective-permute-start | bytes 884744 | tf_op jit(solution)/shard_map/ppermute | solution.py:629
  131.2 6.4 %collective-permute-start.19 = (bf16[2,128,256]{2,1,0:T(8,128)(2,1)S(1)}, bf16[2,128,256]{2,1,0:T(8,128)(2,1)S(1)}, u32[]{:S(2)}, u32[]{:S(2)}) collective-permute-start(bf16[2,128,256]{2,1,0:T(8,128)(2,1)S(1)} %get-tuple-element.95), channel_id=1, source_target_pairs={{0,8},{4,12},{8,0},{12,4},{16,24},{20,28},{24,16},{28,20},{1,9},{5... | collective-permute-start | bytes 393224 | tf_op jit(solution)/shard_map/ppermute | solution.py:629
  138.5 2.4 %collective-permute-done.19 = bf16[2,128,256]{2,1,0:T(8,128)(2,1)S(1)} collective-permute-done((bf16[2,128,256]{2,1,0:T(8,128)(2,1)S(1)}, bf16[2,128,256]{2,1,0:T(8,128)(2,1)S(1)}, u32[]{:S(2)}, u32[]{:S(2)}) %collective-permute-start.19) | collective-permute-done | bytes 131104 | tf_op jit(solution)/shard_map/ppermute | solution.py:629
  141.1 2.1 %collective-permute-done.10 = bf16[2,144,256]{2,1,0:T(8,128)(2,1)S(1)} collective-permute-done((bf16[2,144,256]{2,1,0:T(8,128)(2,1)S(1)}, bf16[2,144,256]{2,1,0:T(8,128)(2,1)S(1)}, u32[]{:S(2)}, u32[]{:S(2)}) %collective-permute-start.10) | collective-permute-done | bytes 147488 | tf_op jit(solution)/shard_map/ppermute | solution.py:629
  143.3 2.8 %collective-permute-done.20 = bf16[1,128,256]{2,1,0:T(8,128)(2,1)S(1)} collective-permute-done((bf16[1,128,256]{2,1,0:T(8,128)(2,1)S(1)}, bf16[1,128,256]{2,1,0:T(8,128)(2,1)S(1)}, u32[]{:S(2)}, u32[]{:S(2)}) %collective-permute-start.20) | collective-permute-done | bytes 65568 | tf_op jit(solution)/shard_map/ppermute | solution.py:629
  146.1 2.2 %collective-permute-done.11 = bf16[1,144,256]{2,1,0:T(8,128)(2,1)S(1)} collective-permute-done((bf16[1,144,256]{2,1,0:T(8,128)(2,1)S(1)}, bf16[1,144,256]{2,1,0:T(8,128)(2,1)S(1)}, u32[]{:S(2)}, u32[]{:S(2)}) %collective-permute-start.11) | collective-permute-done | bytes 73760 | tf_op jit(solution)/shard_map/ppermute | solution.py:629
  149.1 3.6 %collective-permute-done.21 = bf16[1,128,256]{2,1,0:T(8,128)(2,1)S(1)} collective-permute-done((bf16[1,128,256]{2,1,0:T(8,128)(2,1)S(1)}, bf16[1,128,256]{2,1,0:T(8,128)(2,1)S(1)}, u32[]{:S(2)}, u32[]{:S(2)}) %collective-permute-start.21) | collective-permute-done | bytes 65568 | tf_op jit(solution)/shard_map/ppermute | solution.py:629
  153.7 1.3 collective-permute-start.13
  154.9 2.1 %collective-permute-done.22 = bf16[1,128,256]{2,1,0:T(8,128)(2,1)S(1)} collective-permute-done((bf16[1,128,256]{2,1,0:T(8,128)(2,1)S(1)}, bf16[1,128,256]{2,1,0:T(8,128)(2,1)S(1)}, u32[]{:S(2)}, u32[]{:S(2)}) %collective-permute-start.22) | collective-permute-done | bytes 65568 | tf_op jit(solution)/shard_map/ppermute | solution.py:629
  159.5 2.6 %collective-permute-done.23 = bf16[2,128,256]{2,1,0:T(8,128)(2,1)S(1)} collective-permute-done((bf16[2,128,256]{2,1,0:T(8,128)(2,1)S(1)}, bf16[2,128,256]{2,1,0:T(8,128)(2,1)S(1)}, u32[]{:S(2)}, u32[]{:S(2)}) %collective-permute-start.23) | collective-permute-done | bytes 131104 | tf_op jit(solution)/shard_map/ppermute | solution.py:629
  162.9 1.0 collective-permute-done.14
  164.6 3.1 %collective-permute-start.15 = (bf16[4,144,256]{2,1,0:T(8,128)(2,1)S(1)}, bf16[4,144,256]{2,1,0:T(8,128)(2,1)S(1)}, u32[]{:S(2)}, u32[]{:S(2)}) collective-permute-start(bf16[4,144,256]{2,1,0:T(8,128)(2,1)S(1)} %pad_maximum_fusion.2), channel_id=1, source_target_pairs={{0,8},{4,12},{8,0},{12,4},{16,24},{20,28},{24,16},{28,20},{1,9},{5... | collective-permute-start | bytes 884744 | tf_op jit(solution)/shard_map/ppermute | solution.py:629
  167.8 2.5 %collective-permute-done.24 = bf16[4,128,256]{2,1,0:T(8,128)(2,1)S(1)} collective-permute-done((bf16[4,128,256]{2,1,0:T(8,128)(2,1)S(1)}, bf16[4,128,256]{2,1,0:T(8,128)(2,1)S(1)}, u32[]{:S(2)}, u32[]{:S(2)}) %collective-permute-start.24) | collective-permute-done | bytes 262176 | tf_op jit(solution)/shard_map/ppermute | solution.py:629
  170.4 2.0 %collective-permute-done.15 = bf16[4,144,256]{2,1,0:T(8,128)(2,1)S(1)} collective-permute-done((bf16[4,144,256]{2,1,0:T(8,128)(2,1)S(1)}, bf16[4,144,256]{2,1,0:T(8,128)(2,1)S(1)}, u32[]{:S(2)}, u32[]{:S(2)}) %collective-permute-start.15) | collective-permute-done | bytes 294944 | tf_op jit(solution)/shard_map/ppermute | solution.py:629
  173.9 0.9 maximum_add_fusion.1
  176.5 3.9 %shard_map.257 = (f32[2,256,768]{2,1,0:T(8,128)}, f32[2,512]{1,0:T(2,128)}, f32[2,256,256]{2,1,0:T(8,128)}, f32[2,256]{1,0:T(2,128)}, f32[2,256]{1,0:T(2,128)}, ...) custom-call(s32[2]{0:T(128)} %pad_add_fusion.1.refs_0_, ...), custom_call_target="tpu_custom_call" | custom-call | flops 1073741824 | bytes 8388608 | tf_op jit(solution)/shard_map/pallas_call | solution.py:545
  (109 shorter events, 17.2 us)
Async XLA Ops:
  1.8 39.6 %collective-permute-start = (bf16[2,256,256]{2,1,0:T(8,128)(2,1)S(1)}, bf16[2,256,256]{2,1,0:T(8,128)(2,1)S(1)}, u32[]{:S(2)}, u32[]{:S(2)}) collective-permute-start(bf16[2,256,256]{2,1,0:T(8,128)(2,1)S(1)} %get-tuple-element.111), channel_id=1, source_target_pairs={{0,1},{1,0},{2,3},{3,2},{4,5},{5,4},{6,7},{7,6},{8,9},{9,8},{10,11... | collective-permute-start | bytes 786440 | tf_op jit(solution)/shard_map/ppermute | solution.py:594
  4.9 36.5 %collective-permute-start.1 = (bf16[2,256,256]{2,1,0:T(8,128)(2,1)S(1)}, bf16[2,256,256]{2,1,0:T(8,128)(2,1)S(1)}, u32[]{:S(2)}, u32[]{:S(2)}) collective-permute-start(bf16[2,256,256]{2,1,0:T(8,128)(2,1)S(1)} %get-tuple-element.110), channel_id=1, source_target_pairs={{1,2},{2,1},{5,6},{6,5},{9,10},{10,9},{13,14},{14,13},{17,18},{18,... | collective-permute-start | bytes 786440 | tf_op jit(solution)/shard_map/ppermute | solution.py:594
  5.6 11.2 %collective-permute-start.2 = (bf16[2,256,256]{2,1,0:T(8,128)(2,1)S(1)}, bf16[2,256,256]{2,1,0:T(8,128)(2,1)S(1)}, u32[]{:S(2)}, u32[]{:S(2)}) collective-permute-start(bf16[2,256,256]{2,1,0:T(8,128)(2,1)S(1)} %get-tuple-element.107), channel_id=1, source_target_pairs={{0,1},{1,0},{2,3},{3,2},{4,5},{5,4},{6,7},{7,6},{8,9},{9,8},{10,11... | collective-permute-start | bytes 786440 | tf_op jit(solution)/shard_map/ppermute | solution.py:594
  10.1 6.7 %collective-permute-start.3 = (bf16[2,256,256]{2,1,0:T(8,128)(2,1)S(1)}, bf16[2,256,256]{2,1,0:T(8,128)(2,1)S(1)}, u32[]{:S(2)}, u32[]{:S(2)}) collective-permute-start(bf16[2,256,256]{2,1,0:T(8,128)(2,1)S(1)} %get-tuple-element.106), channel_id=1, source_target_pairs={{1,2},{2,1},{5,6},{6,5},{9,10},{10,9},{13,14},{14,13},{17,18},{18,... | collective-permute-start | bytes 786440 | tf_op jit(solution)/shard_map/ppermute | solution.py:594
  85.6 27.0 %collective-permute-start.17 = (bf16[8,128,256]{2,1,0:T(8,128)(2,1)}, bf16[8,128,256]{2,1,0:T(8,128)(2,1)S(1)}, u32[]{:S(2)}, u32[]{:S(2)}) collective-permute-start(bf16[8,128,256]{2,1,0:T(8,128)(2,1)} %get-tuple-element.73), channel_id=1, source_target_pairs={{0,4},{4,0},{8,12},{12,8},{16,20},{20,16},{24,28},{28,24},{1,5},{5... | collective-permute-start | bytes 1572872 | tf_op jit(solution)/shard_map/ppermute | solution.py:629
  112.8 18.3 %collective-permute-start.18 = (bf16[4,128,256]{2,1,0:T(8,128)(2,1)S(1)}, bf16[4,128,256]{2,1,0:T(8,128)(2,1)S(1)}, u32[]{:S(2)}, u32[]{:S(2)}) collective-permute-start(bf16[4,128,256]{2,1,0:T(8,128)(2,1)S(1)} %get-tuple-element.91), channel_id=1, source_target_pairs={{0,16},{4,20},{8,24},{12,28},{16,0},{20,4},{24,8},{28,12},{1,17},{... | collective-permute-start | bytes 786440 | tf_op jit(solution)/shard_map/ppermute | solution.py:629
  114.8 22.8 %collective-permute-start.9 = (bf16[4,144,256]{2,1,0:T(8,128)(2,1)S(1)}, bf16[4,144,256]{2,1,0:T(8,128)(2,1)S(1)}, u32[]{:S(2)}, u32[]{:S(2)}) collective-permute-start(bf16[4,144,256]{2,1,0:T(8,128)(2,1)S(1)} %get-tuple-element.89), channel_id=1, source_target_pairs={{0,8},{4,12},{8,0},{12,4},{16,24},{20,28},{24,16},{28,20},{1,9},{5... | collective-permute-start | bytes 884744 | tf_op jit(solution)/shard_map/ppermute | solution.py:629
  130.4 34.2 %collective-permute-start.4 = (bf16[2,256,256]{2,1,0:T(8,128)(2,1)S(1)}, bf16[2,256,256]{2,1,0:T(8,128)(2,1)S(1)}, u32[]{:S(2)}, u32[]{:S(2)}) collective-permute-start(bf16[2,256,256]{2,1,0:T(8,128)(2,1)S(1)} %get-tuple-element.103), channel_id=1, source_target_pairs={{0,1},{1,0},{2,3},{3,2},{4,5},{5,4},{6,7},{7,6},{8,9},{9,8},{10,11... | collective-permute-start | bytes 786440 | tf_op jit(solution)/shard_map/ppermute | solution.py:594
  130.4 37.3 %collective-permute-start.5 = (bf16[2,256,256]{2,1,0:T(8,128)(2,1)S(1)}, bf16[2,256,256]{2,1,0:T(8,128)(2,1)S(1)}, u32[]{:S(2)}, u32[]{:S(2)}) collective-permute-start(bf16[2,256,256]{2,1,0:T(8,128)(2,1)S(1)} %get-tuple-element.102), channel_id=1, source_target_pairs={{1,2},{2,1},{5,6},{6,5},{9,10},{10,9},{13,14},{14,13},{17,18},{18,... | collective-permute-start | bytes 786440 | tf_op jit(solution)/shard_map/ppermute | solution.py:594
  131.2 9.8 %collective-permute-start.19 = (bf16[2,128,256]{2,1,0:T(8,128)(2,1)S(1)}, bf16[2,128,256]{2,1,0:T(8,128)(2,1)S(1)}, u32[]{:S(2)}, u32[]{:S(2)}) collective-permute-start(bf16[2,128,256]{2,1,0:T(8,128)(2,1)S(1)} %get-tuple-element.95), channel_id=1, source_target_pairs={{0,8},{4,12},{8,0},{12,4},{16,24},{20,28},{24,16},{28,20},{1,9},{5... | collective-permute-start | bytes 393224 | tf_op jit(solution)/shard_map/ppermute | solution.py:629
  137.7 5.4 %collective-permute-start.10 = (bf16[2,144,256]{2,1,0:T(8,128)(2,1)S(1)}, bf16[2,144,256]{2,1,0:T(8,128)(2,1)S(1)}, u32[]{:S(2)}, u32[]{:S(2)}) collective-permute-start(bf16[2,144,256]{2,1,0:T(8,128)(2,1)S(1)} %get-tuple-element.93), channel_id=1, source_target_pairs={{0,16},{4,20},{8,24},{12,28},{16,0},{20,4},{24,8},{28,12},{1,17},{... | collective-permute-start | bytes 442376 | tf_op jit(solution)/shard_map/ppermute | solution.py:629
  141.0 5.0 %collective-permute-start.20 = (bf16[1,128,256]{2,1,0:T(8,128)(2,1)S(1)}, bf16[1,128,256]{2,1,0:T(8,128)(2,1)S(1)}, u32[]{:S(2)}, u32[]{:S(2)}) collective-permute-start(bf16[1,128,256]{2,1,0:T(8,128)(2,1)S(1)} %add_convert_fusion.14), channel_id=1, source_target_pairs={{0,1},{1,0},{2,3},{3,2},{4,5},{5,4},{6,7},{7,6},{8,9},{9,8},{10,11... | collective-permute-start | bytes 196616 | tf_op jit(solution)/shard_map/ppermute | solution.py:629
  143.2 5.1 %collective-permute-start.11 = (bf16[1,144,256]{2,1,0:T(8,128)(2,1)S(1)}, bf16[1,144,256]{2,1,0:T(8,128)(2,1)S(1)}, u32[]{:S(2)}, u32[]{:S(2)}) collective-permute-start(bf16[1,144,256]{2,1,0:T(8,128)(2,1)S(1)} %add_convert_fusion.10), channel_id=1, source_target_pairs={{0,1},{1,0},{2,3},{3,2},{4,5},{5,4},{6,7},{7,6},{8,9},{9,8},{10,11... | collective-permute-start | bytes 221192 | tf_op jit(solution)/shard_map/ppermute | solution.py:629
  146.1 6.7 %collective-permute-start.21 = (bf16[1,128,256]{2,1,0:T(8,128)(2,1)S(1)}, bf16[1,128,256]{2,1,0:T(8,128)(2,1)S(1)}, u32[]{:S(2)}, u32[]{:S(2)}) collective-permute-start(bf16[1,128,256]{2,1,0:T(8,128)(2,1)S(1)} %add_convert_fusion.13), channel_id=1, source_target_pairs={{0,2},{1,3},{2,0},{3,1},{4,6},{5,7},{6,4},{7,5},{8,10},{9,11},{10,... | collective-permute-start | bytes 196616 | tf_op jit(solution)/shard_map/ppermute | solution.py:629
  148.3 5.3 %collective-permute-start.12 = (bf16[1,144,256]{2,1,0:T(8,128)(2,1)S(1)}, bf16[1,144,256]{2,1,0:T(8,128)(2,1)S(1)}, u32[]{:S(2)}, u32[]{:S(2)}) collective-permute-start(bf16[1,144,256]{2,1,0:T(8,128)(2,1)S(1)} %add_convert_fusion.9), channel_id=1, source_target_pairs={{0,2},{1,3},{2,0},{3,1},{4,6},{5,7},{6,4},{7,5},{8,10},{9,11},{10,... | collective-permute-start | bytes 221192 | tf_op jit(solution)/shard_map/ppermute | solution.py:629
  152.8 4.3 %collective-permute-start.22 = (bf16[1,128,256]{2,1,0:T(8,128)(2,1)S(1)}, bf16[1,128,256]{2,1,0:T(8,128)(2,1)S(1)}, u32[]{:S(2)}, u32[]{:S(2)}) collective-permute-start(bf16[1,128,256]{2,1,0:T(8,128)(2,1)S(1)} %add_convert_fusion.12), channel_id=1, source_target_pairs={{0,1},{1,0},{2,3},{3,2},{4,5},{5,4},{6,7},{7,6},{8,9},{9,8},{10,11... | collective-permute-start | bytes 196616 | tf_op jit(solution)/shard_map/ppermute | solution.py:629
  153.7 4.4 %collective-permute-start.13 = (bf16[1,144,256]{2,1,0:T(8,128)(2,1)S(1)}, bf16[1,144,256]{2,1,0:T(8,128)(2,1)S(1)}, u32[]{:S(2)}, u32[]{:S(2)}) collective-permute-start(bf16[1,144,256]{2,1,0:T(8,128)(2,1)S(1)} %add_convert_fusion.8), channel_id=1, source_target_pairs={{0,1},{1,0},{2,3},{3,2},{4,5},{5,4},{6,7},{7,6},{8,9},{9,8},{10,11... | collective-permute-start | bytes 221192 | tf_op jit(solution)/shard_map/ppermute | solution.py:629
  157.1 5.0 %collective-permute-start.23 = (bf16[2,128,256]{2,1,0:T(8,128)(2,1)S(1)}, bf16[2,128,256]{2,1,0:T(8,128)(2,1)S(1)}, u32[]{:S(2)}, u32[]{:S(2)}) collective-permute-start(bf16[2,128,256]{2,1,0:T(8,128)(2,1)S(1)} %pad_maximum_fusion.5), channel_id=1, source_target_pairs={{0,8},{4,12},{8,0},{12,4},{16,24},{20,28},{24,16},{28,20},{1,9},{5... | collective-permute-start | bytes 393224 | tf_op jit(solution)/shard_map/ppermute | solution.py:629
  158.1 5.7 %collective-permute-start.14 = (bf16[2,144,256]{2,1,0:T(8,128)(2,1)S(1)}, bf16[2,144,256]{2,1,0:T(8,128)(2,1)S(1)}, u32[]{:S(2)}, u32[]{:S(2)}) collective-permute-start(bf16[2,144,256]{2,1,0:T(8,128)(2,1)S(1)} %pad_maximum_fusion.4), channel_id=1, source_target_pairs={{0,16},{4,20},{8,24},{12,28},{16,0},{20,4},{24,8},{28,12},{1,17},{... | collective-permute-start | bytes 442376 | tf_op jit(solution)/shard_map/ppermute | solution.py:629
  158.9 14.7 %collective-permute-start.6 = (bf16[2,256,256]{2,1,0:T(8,128)(2,1)S(1)}, bf16[2,256,256]{2,1,0:T(8,128)(2,1)S(1)}, u32[]{:S(2)}, u32[]{:S(2)}) collective-permute-start(bf16[2,256,256]{2,1,0:T(8,128)(2,1)S(1)} %get-tuple-element.99), channel_id=1, source_target_pairs={{0,1},{1,0},{2,3},{3,2},{4,5},{5,4},{6,7},{7,6},{8,9},{9,8},{10,11... | collective-permute-start | bytes 786440 | tf_op jit(solution)/shard_map/ppermute | solution.py:594
  162.1 11.4 %collective-permute-start.7 = (bf16[2,256,256]{2,1,0:T(8,128)(2,1)S(1)}, bf16[2,256,256]{2,1,0:T(8,128)(2,1)S(1)}, u32[]{:S(2)}, u32[]{:S(2)}) collective-permute-start(bf16[2,256,256]{2,1,0:T(8,128)(2,1)S(1)} %get-tuple-element.98), channel_id=1, source_target_pairs={{1,2},{2,1},{5,6},{6,5},{9,10},{10,9},{13,14},{14,13},{17,18},{18,... | collective-permute-start | bytes 786440 | tf_op jit(solution)/shard_map/ppermute | solution.py:594
  163.9 6.4 %collective-permute-start.24 = (bf16[4,128,256]{2,1,0:T(8,128)(2,1)S(1)}, bf16[4,128,256]{2,1,0:T(8,128)(2,1)S(1)}, u32[]{:S(2)}, u32[]{:S(2)}) collective-permute-start(bf16[4,128,256]{2,1,0:T(8,128)(2,1)S(1)} %pad_maximum_fusion.3), channel_id=1, source_target_pairs={{0,16},{4,20},{8,24},{12,28},{16,0},{20,4},{24,8},{28,12},{1,17},{... | collective-permute-start | bytes 786440 | tf_op jit(solution)/shard_map/ppermute | solution.py:629
  164.6 7.8 %collective-permute-start.15 = (bf16[4,144,256]{2,1,0:T(8,128)(2,1)S(1)}, bf16[4,144,256]{2,1,0:T(8,128)(2,1)S(1)}, u32[]{:S(2)}, u32[]{:S(2)}) collective-permute-start(bf16[4,144,256]{2,1,0:T(8,128)(2,1)S(1)} %pad_maximum_fusion.2), channel_id=1, source_target_pairs={{0,8},{4,12},{8,0},{12,4},{16,24},{20,28},{24,16},{28,20},{1,9},{5... | collective-permute-start | bytes 884744 | tf_op jit(solution)/shard_map/ppermute | solution.py:629
  170.3 4.6 %collective-permute-start.25 = (bf16[8,128,256]{2,1,0:T(8,128)(2,1)S(1)}, bf16[8,128,256]{2,1,0:T(8,128)(2,1)S(1)}, u32[]{:S(2)}, u32[]{:S(2)}) collective-permute-start(bf16[8,128,256]{2,1,0:T(8,128)(2,1)S(1)} %pad_maximum_fusion.1.refs_3_), channel_id=1, source_target_pairs={{0,4},{4,0},{8,12},{12,8},{16,20},{20,16},{24,28},{28,24},{1,5},{5... | collective-permute-start | bytes 1572872 | tf_op jit(solution)/shard_map/ppermute | solution.py:629
  (16 other events, 139.8 us)

commit v2 on v1

--- a/solution.py
+++ b/solution.py
@@ -11,8 +11,9 @@
 EPSILON = 1e-12
 MASKED = -1e30
 DOCS = 8
-TB = 256
+TB = 512
 QB = 128
+TURNS = (1, 2, 3, 4)
 LANES = 128
 VMEM_LIMIT = 60 * 1024 * 1024
 
@@ -71,7 +72,7 @@
             return offset + lax.bitwise_and(length + 15, -16), tile + count * count
 
         total, _ = lax.fori_loop(0, items, one, (jnp.int32(0), jnp.int32(0)))
-        self.blocks = lax.shift_right_logical(total + (TB - 1), 8)
+        self.blocks = lax.shift_right_logical(total + (TB - 1), 9)
 
     def start(self, d):
         return self.given[d]
@@ -177,9 +178,17 @@
     return jnp.concatenate([v * masks[0], v * masks[1]], axis=0)
 
 
-def one_of_two(v):
-    lane = lax.broadcasted_iota(jnp.int32, (QB, LANES), 1)
-    return jnp.where(lane < LANES // 2, v[:QB], v[QB:])
+def turned_back(v):
+    row = lax.broadcasted_iota(jnp.int32, (LANES, QB), 0)
+    return jnp.where(row < LANES // 2, v[:, :QB], v[:, QB:]).T
+
+
+def turn(src, dst, width):
+    for k in range(width // LANES):
+        at = slice(k * LANES, (k + 1) * LANES)
+        for g in range(2):
+            here = slice(g * LANES, (g + 1) * LANES)
+            dst[here, at] = src[at, here].T
 
 
 def project(plan, kept, weight, bias):
@@ -198,43 +207,56 @@
     clear(kept.qkv, rows_at(plan.blocks * TB, QB))
 
 
-def attend(plan, most, kept, weights_low):
+def in_turns(count, some):
+    step = TURNS[count - 1]
+    if step == count:
+        some(0, count)
+        return
+
+    def one(k, _):
+        some(k * step, step)
+        return 0
+
+    lax.fori_loop(0, count // step, one, 0)
+
+
+def attend(plan, most, kept, weights_low, values_turned):
     masks = head_masks()
 
     def visit(d, n, length):
         offset, tile = plan.offset(d), plan.tile(d)
         width = n * QB
         keys_at = rows_at(offset, width)
-
-        def one(q, _):
-            queries_at = rows_at(offset + q * QB, QB)
-            row = lax.broadcasted_iota(jnp.int32, (QB, 1), 0) + q * QB
-            row = jnp.concatenate([row, row], axis=0)
-            for g in range(2):
-                cols = g * LANES
-                keys = kept.qkv[keys_at, 256 + cols : 256 + cols + LANES]
-                values = kept.qkv[keys_at, 512 + cols : 512 + cols + LANES]
-                queries = two_heads(kept.qkv[queries_at, cols : cols + LANES], masks)
-                scores = dot_nt(queries, keys)
-                last = scores[:, width - QB :]
-                col = lax.broadcasted_iota(jnp.int32, last.shape, 1)
-                last = jnp.where(col < length - (width - QB), last, MASKED)
-                if n > 1:
-                    scores = jnp.concatenate([scores[:, : width - QB], last], axis=1)
-                else:
-                    scores = last
-                highest = jnp.max(scores, axis=1, keepdims=True)
-                raised = jnp.exp(scores - highest)
-                total = jnp.sum(raised, axis=1, keepdims=True)
-                share = jnp.where(row < length, 1.0 / total, 0.0)
-                probs = (raised * share).astype(BF)
+        turn(kept.qkv[keys_at, 512:768], values_turned, width)
+
+        def some(first, count):
+            column = lax.broadcasted_iota(jnp.int32, (1, 2 * QB), 1)
+            column = lax.bitwise_and(column, QB - 1)
+            row = lax.broadcasted_iota(jnp.int32, (QB, 2 * QB), 0)
+            inside = row < length - (width - QB)
+            chains = [(first + q, g) for q in range(count) for g in range(2)]
+            cols = [slice(g * LANES, (g + 1) * LANES) for g in range(2)]
+            keys = [kept.qkv[keys_at, 256 + c.start : 256 + c.stop] for c in cols]
+            turned = [values_turned[c, :width] for c in cols]
+            queries = [kept.qkv[rows_at(offset + q * QB, QB), cols[g]] for q, g in chains]
+            queries = [two_heads(v, masks) for v in queries]
+            scores = [dot_nt(keys[g], v) for v, (_, g) in zip(queries, chains)]
+            probs = []
+            for v, (q, g) in zip(scores, chains):
+                last = jnp.where(inside, v[width - QB :, :], MASKED)
+                v = jnp.concatenate([v[: width - QB, :], last], axis=0) if n > 1 else last
+                raised = jnp.exp(v - jnp.max(v, axis=0, keepdims=True))
+                total = jnp.sum(raised, axis=0, keepdims=True)
+                share = jnp.where(column + q * QB < length, 1.0 / total, 0.0)
+                probs.append((raised * share).astype(BF))
+            contexts = [dot(turned[g], v) for v, (_, g) in zip(probs, chains)]
+            contexts = [turned_back(v).astype(BF) for v in contexts]
+            for v, context, (q, g) in zip(probs, contexts, chains):
+                kept.ctx[rows_at(offset + q * QB, QB), cols[g]] = context
                 for k in range(n):
-                    weights_low[tile + q * n + k, g] = probs[:, k * QB : (k + 1) * QB]
-                context = one_of_two(dot(probs, values))
-                kept.ctx[queries_at, cols : cols + LANES] = context.astype(BF)
-            return 0
-
-        lax.fori_loop(0, n, one, 0)
+                    weights_low[tile + q * n + k, g] = v[k * QB : (k + 1) * QB, :]
+
+        in_turns(n, some)
 
     plan.over_docs(most, visit)
 
@@ -246,27 +268,36 @@
     return centred * rate, rate
 
 
+def parts_of(b, count):
+    step = TB // count
+    return [rows_at(b * TB + k * step, step) for k in range(count)]
+
+
 def feed(plan, kept, w, out, each=None):
     def visit(b):
-        rows = block(b)
-        x = kept.x[rows, :].astype(F32)
-        attn_sum = x + dot(kept.ctx[rows, :], w.wout[...]) + w.bout[...]
-        n1, r1 = normal(attn_sum)
-        kept.n1[rows, :] = n1.astype(BF)
-        kept.r1[rows, :] = jnp.broadcast_to(r1, (TB, LANES))
-        mid_low = (n1 * w.g1[...] + w.s1[...]).astype(BF)
-        kept.mid[rows, :] = mid_low
-        pre_up = dot(mid_low, w.wup[...]) + w.bup[...]
-        share = 0.5 + 0.5 * lax.erf(pre_up * (0.5**0.5))
-        density = jnp.exp(pre_up * pre_up * -0.5) * 0.3989422804014327
-        active = (pre_up * share).astype(BF)
-        kept.act[rows, :] = active
-        kept.slope[rows, :] = (share + pre_up * density).astype(BF)
-        feed_sum = mid_low.astype(F32) + dot(active, w.wdown[...]) + w.bdown[...]
-        n2, r2 = normal(feed_sum)
-        kept.n2[rows, :] = n2.astype(BF)
-        kept.r2[rows, :] = jnp.broadcast_to(r2, (TB, LANES))
-        out[rows, :] = (n2 * w.g2[...] + w.s2[...]).astype(BF)
+        chains = parts_of(b, 1)
+        wout, wup, wdown = w.wout[...], w.wup[...], w.wdown[...]
+        x = [kept.x[at, :] for at in chains]
+        ctx = [kept.ctx[at, :] for at in chains]
+        attn_sum = [u.astype(F32) + dot(v, wout) + w.bout for u, v in zip(x, ctx)]
+        first = [normal(v) for v in attn_sum]
+        mid_low = [(n * w.g1 + w.s1).astype(BF) for n, _ in first]
+        pre_up = [dot(v, wup) + w.bup for v in mid_low]
+        share = [0.5 + 0.5 * lax.erf(v * (0.5**0.5)) for v in pre_up]
+        active = [(v * p).astype(BF) for v, p in zip(pre_up, share)]
+        density = [jnp.exp(v * v * -0.5) * 0.3989422804014327 for v in pre_up]
+        slope = [(p + v * q).astype(BF) for v, p, q in zip(pre_up, share, density)]
+        feed_sum = [u.astype(F32) + dot(v, wdown) + w.bdown for u, v in zip(mid_low, active)]
+        second = [normal(v) for v in feed_sum]
+        for k, at in enumerate(chains):
+            kept.n1[at, :] = first[k][0].astype(BF)
+            kept.r1[at, :] = jnp.broadcast_to(first[k][1], (at.size, LANES))
+            kept.mid[at, :] = mid_low[k]
+            kept.act[at, :] = active[k]
+            kept.slope[at, :] = slope[k]
+            kept.n2[at, :] = second[k][0].astype(BF)
+            kept.r2[at, :] = jnp.broadcast_to(second[k][1], (at.size, LANES))
+            out[at, :] = (second[k][0] * w.g2 + w.s2).astype(BF)
         if each is not None:
             each(b)
 
@@ -283,39 +314,60 @@
     return (e - jnp.mean(e, axis=1, keepdims=True) - n * inner) * rate
 
 
+def doubled(v):
+    return jnp.concatenate([v, v], axis=1)
+
+
+def joined(values):
+    return jnp.concatenate(values, axis=0) if len(values) > 1 else values[0]
+
+
 def feed_back(plan, kept, w, upstream, r):
     total, small, ctx_grad, sum_grad = r.s_total, r.s_small, r.s_ctx_grad, r.s_sum_grad
 
     def visit(b):
+        chains = parts_of(b, 2)
         rows = block(b)
-        up = upstream[rows, :].astype(F32)
-        n2 = kept.n2[rows, :].astype(F32)
-        small[V_G2] += fold(up * n2)
-        small[V_S2] += fold(up)
-        r2 = kept.r2[rows, :]
-        feed_grad = norm_back(up, n2, jnp.concatenate([r2, r2], axis=1), w.g2[...])
-        low = feed_grad.astype(BF)
-        small[V_DOWN] += fold(low.astype(F32))
-        total[AT_DOWN:AT_ALL, :] += dot_tn(kept.act[rows, :], low)
-        active_grad = dot_nt(low, w.wdown[...])
-        pre_grad = (active_grad * kept.slope[rows, :].astype(F32)).astype(BF)
-        sums = fold(pre_grad.astype(F32))
-        small[V_UP] += sums[:, :256]
-        small[V_UP + 1] += sums[:, 256:]
-        up_grad = dot_tn(kept.mid[rows, :], pre_grad)
-        total[AT_UP : AT_UP + 256, :] += up_grad[:, :256]
-        total[AT_UP + 256 : AT_DOWN, :] += up_grad[:, 256:]
-        mid_grad = (dot_nt(pre_grad, w.wup[...]) + feed_grad).astype(BF).astype(F32)
-        n1 = kept.n1[rows, :].astype(F32)
-        small[V_G1] += fold(mid_grad * n1)
-        small[V_S1] += fold(mid_grad)
-        r1 = kept.r1[rows, :]
-        attn_grad = norm_back(mid_grad, n1, jnp.concatenate([r1, r1], axis=1), w.g1[...])
-        sum_grad[rows, :] = attn_grad
-        low = attn_grad.astype(BF)
-        small[V_OUT] += fold(low.astype(F32))
-        total[AT_OUT:AT_UP, :] += dot_tn(kept.ctx[rows, :], low)
-        ctx_grad[rows, :] = dot_nt(low, w.wout[...]).astype(BF)
+        wout, wup, wdown = w.wout[...], w.wup[...], w.wdown[...]
+        up = [upstream[at, :].astype(F32) for at in chains]
+        n2 = [kept.n2[at, :].astype(F32) for at in chains]
+        r2 = [doubled(kept.r2[at, :]) for at in chains]
+        slope = [kept.slope[at, :] for at in chains]
+        n1 = [kept.n1[at, :].astype(F32) for at in chains]
+        r1 = [doubled(kept.r1[at, :]) for at in chains]
+        act, mid, ctx = kept.act[rows, :], kept.mid[rows, :], kept.ctx[rows, :]
+        feed_grad = [norm_back(u, n, v, w.g2) for u, n, v in zip(up, n2, r2)]
+        feed_low = [v.astype(BF) for v in feed_grad]
+        active_grad = [dot_nt(v, wdown) for v in feed_low]
+        pre_grad = [(v * p.astype(F32)).astype(BF) for v, p in zip(active_grad, slope)]
+        mid_grad = [dot_nt(v, wup) + u for v, u in zip(pre_grad, feed_grad)]
+        mid_grad = [v.astype(BF).astype(F32) for v in mid_grad]
+        attn_grad = [norm_back(u, n, v, w.g1) for u, n, v in zip(mid_grad, n1, r1)]
+        attn_low = [v.astype(BF) for v in attn_grad]
+        back = [dot_nt(v, wout).astype(BF) for v in attn_low]
+        down_total = dot_tn(act, joined(feed_low))
+        up_total = dot_tn(mid, joined(pre_grad))
+        out_total = dot_tn(ctx, joined(attn_low))
+        up_sums = fold(joined(pre_grad).astype(F32))
+        sums = [
+            (V_G2, fold(joined([u * n for u, n in zip(up, n2)]))),
+            (V_S2, fold(joined(up))),
+            (V_DOWN, fold(joined(feed_low).astype(F32))),
+            (V_UP, up_sums[:, :256]),
+            (V_UP + 1, up_sums[:, 256:]),
+            (V_G1, fold(joined([u * n for u, n in zip(mid_grad, n1)]))),
+            (V_S1, fold(joined(mid_grad))),
+            (V_OUT, fold(joined(attn_low).astype(F32))),
+        ]
+        for k, at in enumerate(chains):
+            sum_grad[at, :] = attn_grad[k]
+            ctx_grad[at, :] = back[k]
+        total[AT_DOWN:AT_ALL, :] += down_total
+        total[AT_UP : AT_UP + 256, :] += up_total[:, :256]
+        total[AT_UP + 256 : AT_DOWN, :] += up_total[:, 256:]
+        total[AT_OUT:AT_UP, :] += out_total
+        for line, v in sums:
+            small[line] += v
 
     plan.over_blocks(visit)
     clear(ctx_grad, rows_at(plan.blocks * TB, QB))
@@ -323,7 +375,7 @@
 
 def attend_back(plan, most, kept, r):
     weights_low, ctx_grad, qkv_grad = r.s_probs, r.s_ctx_grad, r.s_qkv_grad
-    key_sums, value_sums = r.s_key_sums, r.s_value_sums
+    key_sums, value_sums, keys_turned = r.s_key_sums, r.s_value_sums, r.s_turned
     masks = head_masks()
     scaling = (256 // HEADS) ** (-0.5)
     plan.over_blocks(lambda b: clear(qkv_grad, block(b)))
@@ -332,31 +384,43 @@
         offset, tile = plan.offset(d), plan.tile(d)
         width = n * QB
         keys_at = rows_at(offset, width)
+        turn(kept.qkv[keys_at, 256:512], keys_turned, width)
         key_sums[:width, :] = jnp.zeros((width, 256), F32)
         value_sums[:width, :] = jnp.zeros((width, 256), F32)
 
-        def one(q, _):
-            queries_at = rows_at(offset + q * QB, QB)
+        def some(first, count):
+            chains = [(first + q, g) for q in range(count) for g in range(2)]
+            cols = [slice(g * LANES, (g + 1) * LANES) for g in range(2)]
+            values = [kept.qkv[keys_at, 512 + c.start : 512 + c.stop] for c in cols]
+            turned = [keys_turned[c, :width] for c in cols]
+            queries = [kept.qkv[rows_at(offset + q * QB, QB), cols[g]] for q, g in chains]
+            grads = [ctx_grad[rows_at(offset + q * QB, QB), cols[g]] for q, g in chains]
+            probs = []
+            for q, g in chains:
+                parts = [weights_low[tile + q * n + k, g] for k in range(n)]
+                probs.append(jnp.concatenate(parts, axis=0) if n > 1 else parts[0])
+            queries = [two_heads(v, masks) for v in queries]
+            grads = [two_heads(v, masks) for v in grads]
+            prob_grads = [dot_nt(values[g], v) for v, (_, g) in zip(grads, chains)]
+            score_grads = []
+            for low, v in zip(probs, prob_grads):
+                full = low.astype(F32)
+                inner = jnp.sum(full * v, axis=0, keepdims=True)
+                score_grads.append((full * (v - inner)).astype(BF))
+            query_grads = [dot(turned[g], v) for v, (_, g) in zip(score_grads, chains)]
+            query_grads = [(turned_back(v) * scaling).astype(BF) for v in query_grads]
             for g in range(2):
-                cols = g * LANES
-                here = slice(cols, cols + LANES)
-                keys = kept.qkv[keys_at, 256 + cols : 256 + cols + LANES]
-                values = kept.qkv[keys_at, 512 + cols : 512 + cols + LANES]
-                queries = two_heads(kept.qkv[queries_at, here], masks)
-                grads = two_heads(ctx_grad[queries_at, here], masks)
-                probs = [weights_low[tile + q * n + k, g] for k in range(n)]
-                probs = jnp.concatenate(probs, axis=1) if n > 1 else probs[0]
-                full = probs.astype(F32)
-                prob_grad = dot_nt(grads, values)
-                inner = jnp.sum(full * prob_grad, axis=1, keepdims=True)
-                score_grad = (full * (prob_grad - inner)).astype(BF)
-                query_grad = one_of_two(dot(score_grad, keys)) * scaling
-                qkv_grad[queries_at, here] = query_grad.astype(BF)
-                key_sums[:width, here] += dot_tn(score_grad, queries)
-                value_sums[:width, here] += dot_tn(probs, grads)
-            return 0
-
-        lax.fori_loop(0, n, one, 0)
+                mine = [i for i, (_, own) in enumerate(chains) if own == g]
+                rows = jnp.concatenate([queries[i] for i in mine], axis=0)
+                sides = jnp.concatenate([score_grads[i] for i in mine], axis=1)
+                key_sums[:width, cols[g]] += dot(sides, rows)
+                rows = jnp.concatenate([grads[i] for i in mine], axis=0)
+                sides = jnp.concatenate([probs[i] for i in mine], axis=1)
+                value_sums[:width, cols[g]] += dot(sides, rows)
+            for v, (q, g) in zip(query_grads, chains):
+                qkv_grad[rows_at(offset + q * QB, QB), cols[g]] = v
+
+        in_turns(n, some)
         qkv_grad[keys_at, 256:512] = key_sums[:width, :].astype(BF)
         qkv_grad[keys_at, 512:768] = value_sums[:width, :].astype(BF)
 
@@ -399,7 +463,7 @@
     project(plan, kept, w.win, w.bin)
     early, late = NAMES[:2], NAMES[2:]
     plan.over_blocks(lambda b: [copy_block(k, b).start() for k in early])
-    attend(plan, most, kept, r.s_probs)
+    attend(plan, most, kept, r.s_probs, r.s_turned)
     plan.over_docs(most, lambda d, n, length: copy_probs(d, n).start())
     feed(plan, kept, w, r.o_next, lambda b: [copy_block(k, b).start() for k in late])
     plan.over_blocks(lambda b: [copy_block(k, b).wait() for k in NAMES])
@@ -411,7 +475,7 @@
     kept = SimpleNamespace(**{k: getattr(r, "s_" + k) for k in NAMES[1:]}, x=r.x)
     w = layer_of(r, layer)
     project(plan, kept, w.win, w.bin)
-    attend(plan, most, kept, r.s_probs)
+    attend(plan, most, kept, r.s_probs, r.s_turned)
     feed(plan, kept, w, r.s_rows)
     unpack(plan, most, r.s_rows, r.s_window, r.o_own, r.o_left, r.o_right, span)
     fill_window(r.s_window, r.own, r.left, r.right, span)
@@ -713,10 +777,11 @@
     token_rows = with_halo(tokens)
     plan = dict(plan=(make_plan(segments, place, section_count), smem))
     kept_scratch = {"s_" + k: pltpu.VMEM((cap, c), t) for k, (c, t) in KEPT.items()}
-    probs_shape = (tiles, 2, 2 * QB, QB)
+    probs_shape = (tiles, 2, QB, 2 * QB)
     kept_scratch.update(
         s_probs=pltpu.VMEM(probs_shape, BF),
         s_window=pltpu.VMEM((row_count * span, features), BF),
+        s_turned=pltpu.VMEM((features, whole), BF),
         s_table=pltpu.SMEM((2 * items,), jnp.int32),
     )
     sems = dict(sems=pltpu.SemaphoreType.DMA((len(NAMES) + 1,)))

time: 183 us -> 150 us (0.82)
  Pallas kernels: 97.2 us -> 58.2 us
  starting transfers between devices: 43.1 us -> 56.1 us
  waiting for transfers between devices: 28.6 us -> 22.8 us
    pallas_call x4, Pallas kernels: 97.2 us -> 58.2 us  [call(): pl.pallas_call(run, out_shape=[jax.ShapeDtypeStruct(s, d) for s, d, _ in...]
    ppermute x8, starting transfers between devices: 10.9 us -> 19.4 us  [swapped(): lax.ppermute(sent, 'pipe', [p for i, j in pairs for p in ((i, j), (j, i))])]
    ppermute x18, waiting for transfers between devices: 24.7 us -> 18.9 us  [exchange(): return lax.ppermute(value, axis, [(i, i ^ stride) for i in range(count)])]
    ppermute x18, starting transfers between devices: 32.2 us -> 36.7 us  [exchange(): return lax.ppermute(value, axis, [(i, i ^ stride) for i in range(count)])]
  transfers between devices with their start and end apart: 26 -> 26, of which waited for: 13 -> 11; matrix products, arithmetic and copies ran while one was open for 4% -> 4% of each run, Pallas kernels for 28% -> 20%
where the time goes in v2:
time: 150 us; the launch traced here: 149 us
  Pallas kernels  58.2 us (39%)
  starting transfers between devices  56.1 us (37%)
  waiting for transfers between devices  22.8 us (15%)
  other arithmetic  7.24 us (5%)
  local copies, waits for them, and re-layouts  3.16 us (2%)
    pallas_call x4, Pallas kernels, call(): pl.pallas_call(run, out_shape=[jax.ShapeDtypeStruct(s, d) for s, d, _ in...  58.2 us
    ppermute x18, starting transfers between devices, exchange(): return lax.ppermute(value, axis, [(i, i ^ stride) for i in range(count)])  36.7 us
    ppermute x8, starting transfers between devices, swapped(): lax.ppermute(sent, 'pipe', [p for i, j in pairs for p in ((i, j), (j, i))])  19.4 us
    ppermute x18, waiting for transfers between devices, exchange(): return lax.ppermute(value, axis, [(i, i ^ stride) for i in range(count)])  18.9 us
    ppermute x8, waiting for transfers between devices, swapped(): lax.ppermute(sent, 'pipe', [p for i, j in pairs for p in ((i, j), (j, i))])  3.91 us
  transfers between devices with their start and end apart: 26, of which 11 were waited for; matrix products, arithmetic and copies ran while one was open for 4% of the time, Pallas kernels for 20%

profile of v2, /device:TPU:0, one launch (start us, length us, event | category | flops | bytes accessed | tf_op | source)
XLA Modules:
  0.0 148.6 jit_solution(2509987159955294953)
XLA Ops:
  1.8 3.1 %collective-permute-start = (bf16[2,256,256]{2,1,0:T(8,128)(2,1)S(1)}, bf16[2,256,256]{2,1,0:T(8,128)(2,1)S(1)}, u32[]{:S(2)}, u32[]{:S(2)}) collective-permute-start(bf16[2,256,256]{2,1,0:T(8,128)(2,1)S(1)} %get-tuple-element.111), channel_id=1, source_target_pairs={{0,1},{1,0},{2,3},{3,2},{4,5},{5,4},{6,7},{7,6},{8,9},{9,8},{10,11... | collective-permute-start | bytes 786440 | tf_op jit(solution)/shard_map/ppermute | solution.py:658
  5.6 4.4 %collective-permute-start.2 = (bf16[2,256,256]{2,1,0:T(8,128)(2,1)S(1)}, bf16[2,256,256]{2,1,0:T(8,128)(2,1)S(1)}, u32[]{:S(2)}, u32[]{:S(2)}) collective-permute-start(bf16[2,256,256]{2,1,0:T(8,128)(2,1)S(1)} %get-tuple-element.107), channel_id=1, source_target_pairs={{0,1},{1,0},{2,3},{3,2},{4,5},{5,4},{6,7},{7,6},{8,9},{9,8},{10,11... | collective-permute-start | bytes 786440 | tf_op jit(solution)/shard_map/ppermute | solution.py:658
  12.9 3.9 %collective-permute-done.2 = bf16[2,256,256]{2,1,0:T(8,128)(2,1)S(1)} collective-permute-done((bf16[2,256,256]{2,1,0:T(8,128)(2,1)S(1)}, bf16[2,256,256]{2,1,0:T(8,128)(2,1)S(1)}, u32[]{:S(2)}, u32[]{:S(2)}) %collective-permute-start.2) | collective-permute-done | bytes 262176 | tf_op jit(solution)/shard_map/ppermute | solution.py:658
  17.6 13.1 %shard_map.254 = (bf16[2560,256]{1,0:T(8,128)(2,1)}, bf16[2560,768]{1,0:T(8,128)(2,1)}, bf16[2560,256]{1,0:T(8,128)(2,1)}, bf16[2560,256]{1,0:T(8,128)(2,1)}, f3...) custom-call(s32[32]{0:T(128)} %reshape.152.refs_0_, ...), custom_call_target="tpu_custom_call" | custom-call | flops 12884901888 | bytes 8388608 | tf_op jit(solution)/shard_map/pallas_call | solution.py:609
  31.6 24.0 %shard_map.255 = (bf16[2,512,256]{2,1,0:T(8,128)(2,1)}, bf16[2,256,256]{2,1,0:T(8,128)(2,1)}, bf16[2,256,256]{2,1,0:T(8,128)(2,1)}, bf16[8,128,256]{2,1,0:T(8,12...) custom-call(s32[32]{0:T(128)} %reshape.152.refs_0_, ...), custom_call_target="tpu_custom_call" | custom-call | flops 38654705664 | bytes 8388608 | tf_op jit(solution)/shard_map/pallas_call | solution.py:609
  55.5 7.1 %collective-permute-start.17 = (bf16[8,128,256]{2,1,0:T(8,128)(2,1)}, bf16[8,128,256]{2,1,0:T(8,128)(2,1)S(1)}, u32[]{:S(2)}, u32[]{:S(2)}) collective-permute-start(bf16[8,128,256]{2,1,0:T(8,128)(2,1)} %get-tuple-element.73), channel_id=1, source_target_pairs={{0,4},{4,0},{8,12},{12,8},{16,20},{20,16},{24,28},{28,24},{1,5},{5... | collective-permute-start | bytes 1572872 | tf_op jit(solution)/shard_map/ppermute | solution.py:693
  62.7 17.3 %shard_map.256 = (bf16[2,512,256]{2,1,0:T(8,128)(2,1)}, bf16[2,256,256]{2,1,0:T(8,128)(2,1)}, bf16[2,256,256]{2,1,0:T(8,128)(2,1)}, bf16[8,144,256]{2,1,0:T(8,128)(2,1)}, bf16[8,144,256]{2,1,0:T(8,128)(2,1)}) custom-call(s32[32]{0:T(128)} %reshape.152.refs_0_, bf16[2560,256]{1,0:T(8,128)(2,1)} %get-tuple-element.54.refs_1_, ...), custom_call_target="tpu_custom_call" | custom-call | flops 25769803776 | bytes 8388608 | tf_op jit(solution)/shard_map/pallas_call | solution.py:609
  80.0 3.5 %collective-permute-start.8 = (bf16[8,144,256]{2,1,0:T(8,128)(2,1)}, bf16[8,144,256]{2,1,0:T(8,128)(2,1)S(1)}, u32[]{:S(2)}, u32[]{:S(2)}) collective-permute-start(bf16[8,144,256]{2,1,0:T(8,128)(2,1)} %get-tuple-element.71), channel_id=1, source_target_pairs={{0,4},{4,0},{8,12},{12,8},{16,20},{20,16},{24,28},{28,24},{1,5},{5... | collective-permute-start | bytes 1769480 | tf_op jit(solution)/shard_map/ppermute | solution.py:693
  84.2 5.5 %collective-permute-start.18 = (bf16[4,128,256]{2,1,0:T(8,128)(2,1)S(1)}, bf16[4,128,256]{2,1,0:T(8,128)(2,1)S(1)}, u32[]{:S(2)}, u32[]{:S(2)}) collective-permute-start(bf16[4,128,256]{2,1,0:T(8,128)(2,1)S(1)} %get-tuple-element.91), channel_id=1, source_target_pairs={{0,16},{4,20},{8,24},{12,28},{16,0},{20,4},{24,8},{28,12},{1,17},{... | collective-permute-start | bytes 786440 | tf_op jit(solution)/shard_map/ppermute | solution.py:693
  90.0 7.1 %collective-permute-start.4 = (bf16[2,256,256]{2,1,0:T(8,128)(2,1)S(1)}, bf16[2,256,256]{2,1,0:T(8,128)(2,1)S(1)}, u32[]{:S(2)}, u32[]{:S(2)}) collective-permute-start(bf16[2,256,256]{2,1,0:T(8,128)(2,1)S(1)} %get-tuple-element.103), channel_id=1, source_target_pairs={{0,1},{1,0},{2,3},{3,2},{4,5},{5,4},{6,7},{7,6},{8,9},{9,8},{10,11... | collective-permute-start | bytes 786440 | tf_op jit(solution)/shard_map/ppermute | solution.py:658
  97.8 2.1 %collective-permute-start.19 = (bf16[2,128,256]{2,1,0:T(8,128)(2,1)S(1)}, bf16[2,128,256]{2,1,0:T(8,128)(2,1)S(1)}, u32[]{:S(2)}, u32[]{:S(2)}) collective-permute-start(bf16[2,128,256]{2,1,0:T(8,128)(2,1)S(1)} %get-tuple-element.95), channel_id=1, source_target_pairs={{0,8},{4,12},{8,0},{12,4},{16,24},{20,28},{24,16},{28,20},{1,9},{5... | collective-permute-start | bytes 393224 | tf_op jit(solution)/shard_map/ppermute | solution.py:693
  101.3 1.8 %collective-permute-done.19 = bf16[2,128,256]{2,1,0:T(8,128)(2,1)S(1)} collective-permute-done((bf16[2,128,256]{2,1,0:T(8,128)(2,1)S(1)}, bf16[2,128,256]{2,1,0:T(8,128)(2,1)S(1)}, u32[]{:S(2)}, u32[]{:S(2)}) %collective-permute-start.19) | collective-permute-done | bytes 131104 | tf_op jit(solution)/shard_map/ppermute | solution.py:693
  103.2 6.0 %collective-permute-start.20 = (bf16[1,128,256]{2,1,0:T(8,128)(2,1)S(1)}, bf16[1,128,256]{2,1,0:T(8,128)(2,1)S(1)}, u32[]{:S(2)}, u32[]{:S(2)}) collective-permute-start(bf16[1,128,256]{2,1,0:T(8,128)(2,1)S(1)} %add_convert_fusion.14), channel_id=1, source_target_pairs={{0,1},{1,0},{2,3},{3,2},{4,5},{5,4},{6,7},{7,6},{8,9},{9,8},{10,11... | collective-permute-start | bytes 196616 | tf_op jit(solution)/shard_map/ppermute | solution.py:693
  109.2 2.2 %collective-permute-start.11 = (bf16[1,144,256]{2,1,0:T(8,128)(2,1)S(1)}, bf16[1,144,256]{2,1,0:T(8,128)(2,1)S(1)}, u32[]{:S(2)}, u32[]{:S(2)}) collective-permute-start(bf16[1,144,256]{2,1,0:T(8,128)(2,1)S(1)} %add_convert_fusion.10), channel_id=1, source_target_pairs={{0,1},{1,0},{2,3},{3,2},{4,5},{5,4},{6,7},{7,6},{8,9},{9,8},{10,11... | collective-permute-start | bytes 221192 | tf_op jit(solution)/shard_map/ppermute | solution.py:693
  112.2 2.2 %collective-permute-done.11 = bf16[1,144,256]{2,1,0:T(8,128)(2,1)S(1)} collective-permute-done((bf16[1,144,256]{2,1,0:T(8,128)(2,1)S(1)}, bf16[1,144,256]{2,1,0:T(8,128)(2,1)S(1)}, u32[]{:S(2)}, u32[]{:S(2)}) %collective-permute-start.11) | collective-permute-done | bytes 73760 | tf_op jit(solution)/shard_map/ppermute | solution.py:693
  115.3 2.9 %collective-permute-done.21 = bf16[1,128,256]{2,1,0:T(8,128)(2,1)S(1)} collective-permute-done((bf16[1,128,256]{2,1,0:T(8,128)(2,1)S(1)}, bf16[1,128,256]{2,1,0:T(8,128)(2,1)S(1)}, u32[]{:S(2)}, u32[]{:S(2)}) %collective-permute-start.21) | collective-permute-done | bytes 65568 | tf_op jit(solution)/shard_map/ppermute | solution.py:693
  119.9 2.2 %collective-permute-start.13 = (bf16[1,144,256]{2,1,0:T(8,128)(2,1)S(1)}, bf16[1,144,256]{2,1,0:T(8,128)(2,1)S(1)}, u32[]{:S(2)}, u32[]{:S(2)}) collective-permute-start(bf16[1,144,256]{2,1,0:T(8,128)(2,1)S(1)} %add_convert_fusion.8), channel_id=1, source_target_pairs={{0,1},{1,0},{2,3},{3,2},{4,5},{5,4},{6,7},{7,6},{8,9},{9,8},{10,11... | collective-permute-start | bytes 221192 | tf_op jit(solution)/shard_map/ppermute | solution.py:693
  122.6 2.1 %collective-permute-done.13 = bf16[1,144,256]{2,1,0:T(8,128)(2,1)S(1)} collective-permute-done((bf16[1,144,256]{2,1,0:T(8,128)(2,1)S(1)}, bf16[1,144,256]{2,1,0:T(8,128)(2,1)S(1)}, u32[]{:S(2)}, u32[]{:S(2)}) %collective-permute-start.13) | collective-permute-done | bytes 73760 | tf_op jit(solution)/shard_map/ppermute | solution.py:693
  124.7 2.2 %collective-permute-start.14 = (bf16[2,144,256]{2,1,0:T(8,128)(2,1)S(1)}, bf16[2,144,256]{2,1,0:T(8,128)(2,1)S(1)}, u32[]{:S(2)}, u32[]{:S(2)}) collective-permute-start(bf16[2,144,256]{2,1,0:T(8,128)(2,1)S(1)} %pad_maximum_fusion.4), channel_id=1, source_target_pairs={{0,16},{4,20},{8,24},{12,28},{16,0},{20,4},{24,8},{28,12},{1,17},{... | collective-permute-start | bytes 442376 | tf_op jit(solution)/shard_map/ppermute | solution.py:693
  127.0 2.1 %collective-permute-start.6 = (bf16[2,256,256]{2,1,0:T(8,128)(2,1)S(1)}, bf16[2,256,256]{2,1,0:T(8,128)(2,1)S(1)}, u32[]{:S(2)}, u32[]{:S(2)}) collective-permute-start(bf16[2,256,256]{2,1,0:T(8,128)(2,1)S(1)} %get-tuple-element.99), channel_id=1, source_target_pairs={{0,1},{1,0},{2,3},{3,2},{4,5},{5,4},{6,7},{7,6},{8,9},{9,8},{10,11... | collective-permute-start | bytes 786440 | tf_op jit(solution)/shard_map/ppermute | solution.py:658
  131.6 2.1 %collective-permute-start.24 = (bf16[4,128,256]{2,1,0:T(8,128)(2,1)S(1)}, bf16[4,128,256]{2,1,0:T(8,128)(2,1)S(1)}, u32[]{:S(2)}, u32[]{:S(2)}) collective-permute-start(bf16[4,128,256]{2,1,0:T(8,128)(2,1)S(1)} %pad_maximum_fusion.3), channel_id=1, source_target_pairs={{0,16},{4,20},{8,24},{12,28},{16,0},{20,4},{24,8},{28,12},{1,17},{... | collective-permute-start | bytes 786440 | tf_op jit(solution)/shard_map/ppermute | solution.py:693
  133.9 4.1 %collective-permute-done.24 = bf16[4,128,256]{2,1,0:T(8,128)(2,1)S(1)} collective-permute-done((bf16[4,128,256]{2,1,0:T(8,128)(2,1)S(1)}, bf16[4,128,256]{2,1,0:T(8,128)(2,1)S(1)}, u32[]{:S(2)}, u32[]{:S(2)}) %collective-permute-start.24) | collective-permute-done | bytes 262176 | tf_op jit(solution)/shard_map/ppermute | solution.py:693
  138.2 2.3 %collective-permute-done.15 = bf16[4,144,256]{2,1,0:T(8,128)(2,1)S(1)} collective-permute-done((bf16[4,144,256]{2,1,0:T(8,128)(2,1)S(1)}, bf16[4,144,256]{2,1,0:T(8,128)(2,1)S(1)}, u32[]{:S(2)}, u32[]{:S(2)}) %collective-permute-start.15) | collective-permute-done | bytes 294944 | tf_op jit(solution)/shard_map/ppermute | solution.py:693
  144.7 3.9 %shard_map.257 = (f32[2,256,768]{2,1,0:T(8,128)}, f32[2,512]{1,0:T(2,128)}, f32[2,256,256]{2,1,0:T(8,128)}, f32[2,256]{1,0:T(2,128)}, f32[2,256]{1,0:T(2,128)}, ...) custom-call(s32[2]{0:T(128)} %pad_add_fusion.1.refs_0_, ...), custom_call_target="tpu_custom_call" | custom-call | flops 1073741824 | bytes 8388608 | tf_op jit(solution)/shard_map/pallas_call | solution.py:609
  (109 shorter events, 20.4 us)
Async XLA Ops:
  1.8 28.9 %collective-permute-start = (bf16[2,256,256]{2,1,0:T(8,128)(2,1)S(1)}, bf16[2,256,256]{2,1,0:T(8,128)(2,1)S(1)}, u32[]{:S(2)}, u32[]{:S(2)}) collective-permute-start(bf16[2,256,256]{2,1,0:T(8,128)(2,1)S(1)} %get-tuple-element.111), channel_id=1, source_target_pairs={{0,1},{1,0},{2,3},{3,2},{4,5},{5,4},{6,7},{7,6},{8,9},{9,8},{10,11... | collective-permute-start | bytes 786440 | tf_op jit(solution)/shard_map/ppermute | solution.py:658
  4.9 25.9 %collective-permute-start.1 = (bf16[2,256,256]{2,1,0:T(8,128)(2,1)S(1)}, bf16[2,256,256]{2,1,0:T(8,128)(2,1)S(1)}, u32[]{:S(2)}, u32[]{:S(2)}) collective-permute-start(bf16[2,256,256]{2,1,0:T(8,128)(2,1)S(1)} %get-tuple-element.110), channel_id=1, source_target_pairs={{1,2},{2,1},{5,6},{6,5},{9,10},{10,9},{13,14},{14,13},{17,18},{18,... | collective-permute-start | bytes 786440 | tf_op jit(solution)/shard_map/ppermute | solution.py:658
  5.6 11.2 %collective-permute-start.2 = (bf16[2,256,256]{2,1,0:T(8,128)(2,1)S(1)}, bf16[2,256,256]{2,1,0:T(8,128)(2,1)S(1)}, u32[]{:S(2)}, u32[]{:S(2)}) collective-permute-start(bf16[2,256,256]{2,1,0:T(8,128)(2,1)S(1)} %get-tuple-element.107), channel_id=1, source_target_pairs={{0,1},{1,0},{2,3},{3,2},{4,5},{5,4},{6,7},{7,6},{8,9},{9,8},{10,11... | collective-permute-start | bytes 786440 | tf_op jit(solution)/shard_map/ppermute | solution.py:658
  10.1 6.7 %collective-permute-start.3 = (bf16[2,256,256]{2,1,0:T(8,128)(2,1)S(1)}, bf16[2,256,256]{2,1,0:T(8,128)(2,1)S(1)}, u32[]{:S(2)}, u32[]{:S(2)}) collective-permute-start(bf16[2,256,256]{2,1,0:T(8,128)(2,1)S(1)} %get-tuple-element.106), channel_id=1, source_target_pairs={{1,2},{2,1},{5,6},{6,5},{9,10},{10,9},{13,14},{14,13},{17,18},{18,... | collective-permute-start | bytes 786440 | tf_op jit(solution)/shard_map/ppermute | solution.py:658
  55.5 28.5 %collective-permute-start.17 = (bf16[8,128,256]{2,1,0:T(8,128)(2,1)}, bf16[8,128,256]{2,1,0:T(8,128)(2,1)S(1)}, u32[]{:S(2)}, u32[]{:S(2)}) collective-permute-start(bf16[8,128,256]{2,1,0:T(8,128)(2,1)} %get-tuple-element.73), channel_id=1, source_target_pairs={{0,4},{4,0},{8,12},{12,8},{16,20},{20,16},{24,28},{28,24},{1,5},{5... | collective-permute-start | bytes 1572872 | tf_op jit(solution)/shard_map/ppermute | solution.py:693
  80.0 9.7 %collective-permute-start.8 = (bf16[8,144,256]{2,1,0:T(8,128)(2,1)}, bf16[8,144,256]{2,1,0:T(8,128)(2,1)S(1)}, u32[]{:S(2)}, u32[]{:S(2)}) collective-permute-start(bf16[8,144,256]{2,1,0:T(8,128)(2,1)} %get-tuple-element.71), channel_id=1, source_target_pairs={{0,4},{4,0},{8,12},{12,8},{16,20},{20,16},{24,28},{28,24},{1,5},{5... | collective-permute-start | bytes 1769480 | tf_op jit(solution)/shard_map/ppermute | solution.py:693
  84.2 13.5 %collective-permute-start.18 = (bf16[4,128,256]{2,1,0:T(8,128)(2,1)S(1)}, bf16[4,128,256]{2,1,0:T(8,128)(2,1)S(1)}, u32[]{:S(2)}, u32[]{:S(2)}) collective-permute-start(bf16[4,128,256]{2,1,0:T(8,128)(2,1)S(1)} %get-tuple-element.91), channel_id=1, source_target_pairs={{0,16},{4,20},{8,24},{12,28},{16,0},{20,4},{24,8},{28,12},{1,17},{... | collective-permute-start | bytes 786440 | tf_op jit(solution)/shard_map/ppermute | solution.py:693
  89.8 10.0 %collective-permute-start.9 = (bf16[4,144,256]{2,1,0:T(8,128)(2,1)S(1)}, bf16[4,144,256]{2,1,0:T(8,128)(2,1)S(1)}, u32[]{:S(2)}, u32[]{:S(2)}) collective-permute-start(bf16[4,144,256]{2,1,0:T(8,128)(2,1)S(1)} %get-tuple-element.89), channel_id=1, source_target_pairs={{0,8},{4,12},{8,0},{12,4},{16,24},{20,28},{24,16},{28,20},{1,9},{5... | collective-permute-start | bytes 884744 | tf_op jit(solution)/shard_map/ppermute | solution.py:693
  90.0 43.8 %collective-permute-start.4 = (bf16[2,256,256]{2,1,0:T(8,128)(2,1)S(1)}, bf16[2,256,256]{2,1,0:T(8,128)(2,1)S(1)}, u32[]{:S(2)}, u32[]{:S(2)}) collective-permute-start(bf16[2,256,256]{2,1,0:T(8,128)(2,1)S(1)} %get-tuple-element.103), channel_id=1, source_target_pairs={{0,1},{1,0},{2,3},{3,2},{4,5},{5,4},{6,7},{7,6},{8,9},{9,8},{10,11... | collective-permute-start | bytes 786440 | tf_op jit(solution)/shard_map/ppermute | solution.py:658
  97.0 36.8 %collective-permute-start.5 = (bf16[2,256,256]{2,1,0:T(8,128)(2,1)S(1)}, bf16[2,256,256]{2,1,0:T(8,128)(2,1)S(1)}, u32[]{:S(2)}, u32[]{:S(2)}) collective-permute-start(bf16[2,256,256]{2,1,0:T(8,128)(2,1)S(1)} %get-tuple-element.102), channel_id=1, source_target_pairs={{1,2},{2,1},{5,6},{6,5},{9,10},{10,9},{13,14},{14,13},{17,18},{18,... | collective-permute-start | bytes 786440 | tf_op jit(solution)/shard_map/ppermute | solution.py:658
  97.8 5.4 %collective-permute-start.19 = (bf16[2,128,256]{2,1,0:T(8,128)(2,1)S(1)}, bf16[2,128,256]{2,1,0:T(8,128)(2,1)S(1)}, u32[]{:S(2)}, u32[]{:S(2)}) collective-permute-start(bf16[2,128,256]{2,1,0:T(8,128)(2,1)S(1)} %get-tuple-element.95), channel_id=1, source_target_pairs={{0,8},{4,12},{8,0},{12,4},{16,24},{20,28},{24,16},{28,20},{1,9},{5... | collective-permute-start | bytes 393224 | tf_op jit(solution)/shard_map/ppermute | solution.py:693
  99.9 9.2 %collective-permute-start.10 = (bf16[2,144,256]{2,1,0:T(8,128)(2,1)S(1)}, bf16[2,144,256]{2,1,0:T(8,128)(2,1)S(1)}, u32[]{:S(2)}, u32[]{:S(2)}) collective-permute-start(bf16[2,144,256]{2,1,0:T(8,128)(2,1)S(1)} %get-tuple-element.93), channel_id=1, source_target_pairs={{0,16},{4,20},{8,24},{12,28},{16,0},{20,4},{24,8},{28,12},{1,17},{... | collective-permute-start | bytes 442376 | tf_op jit(solution)/shard_map/ppermute | solution.py:693
  103.2 8.9 %collective-permute-start.20 = (bf16[1,128,256]{2,1,0:T(8,128)(2,1)S(1)}, bf16[1,128,256]{2,1,0:T(8,128)(2,1)S(1)}, u32[]{:S(2)}, u32[]{:S(2)}) collective-permute-start(bf16[1,128,256]{2,1,0:T(8,128)(2,1)S(1)} %add_convert_fusion.14), channel_id=1, source_target_pairs={{0,1},{1,0},{2,3},{3,2},{4,5},{5,4},{6,7},{7,6},{8,9},{9,8},{10,11... | collective-permute-start | bytes 196616 | tf_op jit(solution)/shard_map/ppermute | solution.py:693
  109.2 5.2 %collective-permute-start.11 = (bf16[1,144,256]{2,1,0:T(8,128)(2,1)S(1)}, bf16[1,144,256]{2,1,0:T(8,128)(2,1)S(1)}, u32[]{:S(2)}, u32[]{:S(2)}) collective-permute-start(bf16[1,144,256]{2,1,0:T(8,128)(2,1)S(1)} %add_convert_fusion.10), channel_id=1, source_target_pairs={{0,1},{1,0},{2,3},{3,2},{4,5},{5,4},{6,7},{7,6},{8,9},{9,8},{10,11... | collective-permute-start | bytes 221192 | tf_op jit(solution)/shard_map/ppermute | solution.py:693
  112.2 6.0 %collective-permute-start.21 = (bf16[1,128,256]{2,1,0:T(8,128)(2,1)S(1)}, bf16[1,128,256]{2,1,0:T(8,128)(2,1)S(1)}, u32[]{:S(2)}, u32[]{:S(2)}) collective-permute-start(bf16[1,128,256]{2,1,0:T(8,128)(2,1)S(1)} %add_convert_fusion.13), channel_id=1, source_target_pairs={{0,2},{1,3},{2,0},{3,1},{4,6},{5,7},{6,4},{7,5},{8,10},{9,11},{10,... | collective-permute-start | bytes 196616 | tf_op jit(solution)/shard_map/ppermute | solution.py:693
  114.5 5.4 %collective-permute-start.12 = (bf16[1,144,256]{2,1,0:T(8,128)(2,1)S(1)}, bf16[1,144,256]{2,1,0:T(8,128)(2,1)S(1)}, u32[]{:S(2)}, u32[]{:S(2)}) collective-permute-start(bf16[1,144,256]{2,1,0:T(8,128)(2,1)S(1)} %add_convert_fusion.9), channel_id=1, source_target_pairs={{0,2},{1,3},{2,0},{3,1},{4,6},{5,7},{6,4},{7,5},{8,10},{9,11},{10,... | collective-permute-start | bytes 221192 | tf_op jit(solution)/shard_map/ppermute | solution.py:693
  119.9 4.8 %collective-permute-start.13 = (bf16[1,144,256]{2,1,0:T(8,128)(2,1)S(1)}, bf16[1,144,256]{2,1,0:T(8,128)(2,1)S(1)}, u32[]{:S(2)}, u32[]{:S(2)}) collective-permute-start(bf16[1,144,256]{2,1,0:T(8,128)(2,1)S(1)} %add_convert_fusion.8), channel_id=1, source_target_pairs={{0,1},{1,0},{2,3},{3,2},{4,5},{5,4},{6,7},{7,6},{8,9},{9,8},{10,11... | collective-permute-start | bytes 221192 | tf_op jit(solution)/shard_map/ppermute | solution.py:693
  122.5 6.7 %collective-permute-start.23 = (bf16[2,128,256]{2,1,0:T(8,128)(2,1)S(1)}, bf16[2,128,256]{2,1,0:T(8,128)(2,1)S(1)}, u32[]{:S(2)}, u32[]{:S(2)}) collective-permute-start(bf16[2,128,256]{2,1,0:T(8,128)(2,1)S(1)} %pad_maximum_fusion.5), channel_id=1, source_target_pairs={{0,8},{4,12},{8,0},{12,4},{16,24},{20,28},{24,16},{28,20},{1,9},{5... | collective-permute-start | bytes 393224 | tf_op jit(solution)/shard_map/ppermute | solution.py:693
  124.7 6.9 %collective-permute-start.14 = (bf16[2,144,256]{2,1,0:T(8,128)(2,1)S(1)}, bf16[2,144,256]{2,1,0:T(8,128)(2,1)S(1)}, u32[]{:S(2)}, u32[]{:S(2)}) collective-permute-start(bf16[2,144,256]{2,1,0:T(8,128)(2,1)S(1)} %pad_maximum_fusion.4), channel_id=1, source_target_pairs={{0,16},{4,20},{8,24},{12,28},{16,0},{20,4},{24,8},{28,12},{1,17},{... | collective-permute-start | bytes 442376 | tf_op jit(solution)/shard_map/ppermute | solution.py:693
  127.0 14.6 %collective-permute-start.6 = (bf16[2,256,256]{2,1,0:T(8,128)(2,1)S(1)}, bf16[2,256,256]{2,1,0:T(8,128)(2,1)S(1)}, u32[]{:S(2)}, u32[]{:S(2)}) collective-permute-start(bf16[2,256,256]{2,1,0:T(8,128)(2,1)S(1)} %get-tuple-element.99), channel_id=1, source_target_pairs={{0,1},{1,0},{2,3},{3,2},{4,5},{5,4},{6,7},{7,6},{8,9},{9,8},{10,11... | collective-permute-start | bytes 786440 | tf_op jit(solution)/shard_map/ppermute | solution.py:658
  129.2 12.5 %collective-permute-start.7 = (bf16[2,256,256]{2,1,0:T(8,128)(2,1)S(1)}, bf16[2,256,256]{2,1,0:T(8,128)(2,1)S(1)}, u32[]{:S(2)}, u32[]{:S(2)}) collective-permute-start(bf16[2,256,256]{2,1,0:T(8,128)(2,1)S(1)} %get-tuple-element.98), channel_id=1, source_target_pairs={{1,2},{2,1},{5,6},{6,5},{9,10},{10,9},{13,14},{14,13},{17,18},{18,... | collective-permute-start | bytes 786440 | tf_op jit(solution)/shard_map/ppermute | solution.py:658
  131.6 6.4 %collective-permute-start.24 = (bf16[4,128,256]{2,1,0:T(8,128)(2,1)S(1)}, bf16[4,128,256]{2,1,0:T(8,128)(2,1)S(1)}, u32[]{:S(2)}, u32[]{:S(2)}) collective-permute-start(bf16[4,128,256]{2,1,0:T(8,128)(2,1)S(1)} %pad_maximum_fusion.3), channel_id=1, source_target_pairs={{0,16},{4,20},{8,24},{12,28},{16,0},{20,4},{24,8},{28,12},{1,17},{... | collective-permute-start | bytes 786440 | tf_op jit(solution)/shard_map/ppermute | solution.py:693
  133.8 6.8 %collective-permute-start.15 = (bf16[4,144,256]{2,1,0:T(8,128)(2,1)S(1)}, bf16[4,144,256]{2,1,0:T(8,128)(2,1)S(1)}, u32[]{:S(2)}, u32[]{:S(2)}) collective-permute-start(bf16[4,144,256]{2,1,0:T(8,128)(2,1)S(1)} %pad_maximum_fusion.2), channel_id=1, source_target_pairs={{0,8},{4,12},{8,0},{12,4},{16,24},{20,28},{24,16},{28,20},{1,9},{5... | collective-permute-start | bytes 884744 | tf_op jit(solution)/shard_map/ppermute | solution.py:693
  138.1 4.9 %collective-permute-start.25 = (bf16[8,128,256]{2,1,0:T(8,128)(2,1)S(1)}, bf16[8,128,256]{2,1,0:T(8,128)(2,1)S(1)}, u32[]{:S(2)}, u32[]{:S(2)}) collective-permute-start(bf16[8,128,256]{2,1,0:T(8,128)(2,1)S(1)} %pad_maximum_fusion.1.refs_3_), channel_id=1, source_target_pairs={{0,4},{4,0},{8,12},{12,8},{16,20},{20,16},{24,28},{28,24},{1,5},{5... | collective-permute-start | bytes 1572872 | tf_op jit(solution)/shard_map/ppermute | solution.py:693
  (16 other events, 133.2 us)
